TPU v7x, 256 devices: a whole 4x4x8 slice. The times are simulated.
256 devices in a mesh: ci: 8 (over z), co: 16 (over y, x_hi, core), sp: 2 (over x_lo).
Axes of the slice: x: 4 (x_hi: 2, x_lo: 2; x = x_hi * 2 + x_lo), y: 4, z: 8, core: 2. Of those that a mesh axis runs over, the one named last changes fastest.
Arguments:
- features: bfloat16 [32, 512, 256], P(None, 'ci', 'sp'), may hold values from -6 to 6
- weight: bfloat16 [27, 512, 512], P(None, 'ci', 'co'), may hold values from -0.0546875 to 0.0546875
- bias_vector: float32 [512], P('co'), may hold values from -3 to 3
- cotangent: bfloat16 [32, 512, 256], P('ci', 'co', 'sp'), may hold values from -6 to 6
Outputs:
- activated: bfloat16 [32, 512, 256], P('ci', 'co', 'sp')
- input_grad: float32 [32, 512, 256], P('co', 'ci', 'sp')
- weight_grad: float32 [27, 512, 512], P(None, 'ci', 'co')
- bias_grad: float32 [512], P('co')
All inputs are finite; a program needn't handle non-finite values.
Results may differ from a plain program's by a relative error of at most 0.02.
Values may be sent and summed in bfloat16 or wider, within the bound.
No kernel may reach another device: no remote copies, remote signals or barrier semaphores. Data moves between devices by JAX's collectives and lax.ppermute only.
A program may use at most 64 MiB of HBM per device.

v0:
```python
import jax
import jax.numpy as jnp
from jax import lax
from jax.experimental import pallas as pl
from jax.experimental.pallas import tpu as pltpu
from jax.sharding import PartitionSpec as P

SZ = 32
LANES = 128
BF16 = jnp.bfloat16
F32 = jnp.float32
VMEM = pl.BlockSpec(memory_space=pltpu.VMEM)
SMEM = pl.BlockSpec(memory_space=pltpu.SMEM)


def call(body, outs, specs, flops, moved, scratch=()):
    return pl.pallas_call(
        body,
        out_shape=outs,
        in_specs=specs,
        out_specs=jax.tree.map(lambda _: VMEM, outs),
        scratch_shapes=list(scratch),
        cost_estimate=pl.CostEstimate(flops=flops, bytes_accessed=moved, transcendentals=0),
        compiler_params=pltpu.CompilerParams(vmem_limit_bytes=40 * 2**20),
    )


def lane(shape):
    return lax.broadcasted_iota(jnp.int32, shape, len(shape) - 1)


def pack_plane(side, planes):
    packed = None
    at = lane(planes[0].shape)
    for k, plane in enumerate(planes):
        moved = pltpu.roll(plane, lax.rem(SZ * k + SZ * (1 - side), LANES), 1)
        packed = moved if packed is None else jnp.where(at >= SZ * k, moved, packed)
    return packed


def neighbours(own, low, high, k):
    at = lane(own.shape)
    before = jnp.where(at < SZ, pltpu.roll(low, (-SZ * k) % LANES, 1), pltpu.roll(own, SZ, 1))
    after = jnp.where(
        at >= LANES - SZ,
        pltpu.roll(high, (LANES - SZ - SZ * k) % LANES, 1),
        pltpu.roll(own, LANES - SZ, 1),
    )
    return before, own, after


def split_halo(side, packed):
    zero = jnp.zeros_like(packed)
    return jnp.where(side == 1, packed, zero), jnp.where(side == 0, packed, zero)


def along_z(terms):
    lower, middle, upper = terms
    width = middle.shape[1]
    z = lane((middle.shape[0], LANES)) % SZ
    parts = []
    for start in range(0, width, LANES):
        cut = slice(start, start + LANES)
        parts.append(
            middle[:, cut]
            + jnp.where(z == 0, 0.0, pltpu.roll(lower[:, cut], 1, 1))
            + jnp.where(z == SZ - 1, 0.0, pltpu.roll(upper[:, cut], LANES - 1, 1))
        )
    return parts


def pack_features(side_ref, features_ref, out_ref):
    side = side_ref[0]
    for group in range(out_ref.shape[0]):
        out_ref[group] = pack_plane(side, [features_ref[4 * group + k] for k in range(4)])


def correlate(taps_ref, spread_ref, rows_y, width, store):
    depth = 3 * spread_ref.shape[1]
    taps = taps_ref[...]
    for y in range(0, rows_y, 2):
        columns = jnp.concatenate(
            [spread_ref[y + k : y + k + 3].reshape(depth, LANES) for k in range(2)], axis=1
        )
        product = jnp.dot(taps, columns, preferred_element_type=F32)
        parts = along_z([product[c * width : (c + 1) * width] for c in range(3)])
        for k in range(2):
            store(y + k, parts[k].astype(BF16))


def forward(side_ref, features_ref, halo_ref, weight_ref, out_ref, spread_ref, taps_ref):
    rows_y, width_in, _ = features_ref.shape
    width_out = weight_ref.shape[1]
    side = side_ref[0]
    blank = jnp.zeros(spread_ref.shape[1:], BF16)
    spread_ref[0] = blank
    spread_ref[rows_y + 1] = blank
    for group in range(rows_y // 4):
        low, high = split_halo(side, halo_ref[group])
        for k in range(4):
            y = 4 * group + k
            seen = neighbours(features_ref[y], low, high, k)
            for b in range(3):
                spread_ref[y + 1, b * width_in : (b + 1) * width_in] = seen[b]
    for c in range(3):
        taps_ref[c * width_out : (c + 1) * width_out] = jnp.concatenate(
            [weight_ref[3 * ab + c] for ab in range(9)], axis=1
        )

    def store(y, value):
        out_ref[y] = value

    correlate(taps_ref, spread_ref, rows_y, width_out, store)


def pointwise(side_ref, partial_ref, bias_ref, cotangent_ref, act_ref, grad_ref, edge_ref):
    total = partial_ref[0].astype(F32)
    for k in range(1, partial_ref.shape[0]):
        total = total + partial_ref[k].astype(F32)
    pre = total + bias_ref[...][None]
    scale, cubic = 0.7978845608, 0.044715
    square = pre * pre
    bend = jnp.tanh(scale * (pre + cubic * (square * pre)))
    half = 0.5 * (1.0 + bend)
    act_ref[...] = (pre * half).astype(BF16)
    slope = half + 0.5 * pre * (1.0 - bend * bend) * (scale * (1.0 + 3.0 * cubic * square))
    grad = (cotangent_ref[...].astype(F32) * slope).astype(BF16)
    grad_ref[...] = grad
    edge_ref[...] = pack_plane(side_ref[0], [grad[k] for k in range(4)])


def replicate(grad_ref, halo_ref, out_ref):
    rows = grad_ref.shape[0] * grad_ref.shape[1]
    own = grad_ref[...].reshape(rows, LANES)
    for k in range(out_ref.shape[0]):
        out_ref[k, :rows] = own
        out_ref[k, rows:] = halo_ref[...]


def spread_gradient(side, gathered_ref, width, put):
    rows = 4 * width
    for group in range(gathered_ref.shape[0]):
        low, high = split_halo(side, gathered_ref[group, rows:])
        for k in range(4):
            own = gathered_ref[group, k * width : (k + 1) * width]
            put(4 * group + k, neighbours(own, low, high, k))


def backward(side_ref, gathered_ref, weight_ref, out_ref, spread_ref, taps_ref):
    rows_y, width_in, _ = out_ref.shape
    width_out = weight_ref.shape[1]
    blank = jnp.zeros(spread_ref.shape[1:], BF16)
    spread_ref[0] = blank
    spread_ref[rows_y + 1] = blank

    def put(y, seen):
        for b in range(3):
            spread_ref[y + 1, b * width_out : (b + 1) * width_out] = seen[b]

    spread_gradient(side_ref[0], gathered_ref, width_out, put)
    for c in range(3):
        block = jnp.concatenate([weight_ref[26 - 3 * ab - c] for ab in range(9)], axis=0)
        taps_ref[c * width_in : (c + 1) * width_in] = block.T

    def store(y, value):
        out_ref[y] = value

    correlate(taps_ref, spread_ref, rows_y, width_in, store)


def filter_gradient(side_ref, features_ref, gathered_ref, out_ref, grad_ref, rows_ref):
    rows_y, width_in, _ = features_ref.shape
    width_out = grad_ref.shape[0] // 9
    z = lane((width_out, LANES)) % SZ
    zero = jnp.zeros((width_out, LANES), BF16)

    def put(y, seen):
        columns = slice(y * LANES, (y + 1) * LANES)
        for b in range(3):
            own = seen[2 - b]
            moved = (
                jnp.where(z == SZ - 1, zero, pltpu.roll(own, LANES - 1, 1)),
                own,
                jnp.where(z == 0, zero, pltpu.roll(own, 1, 1)),
            )
            for c in range(3):
                start = (3 * b + c) * width_out
                grad_ref[start : start + width_out, columns] = moved[c]

    spread_gradient(side_ref[0], gathered_ref, width_out, put)
    for a in range(3):
        for y in range(rows_y):
            source = y + a - 1
            inside = 0 <= source < rows_y
            rows_ref[a * width_in : (a + 1) * width_in, y * LANES : (y + 1) * LANES] = (
                features_ref[source] if inside else jnp.zeros((width_in, LANES), BF16)
            )
    over_voxels = (((1,), (1,)), ((), ()))
    grads = grad_ref[...]
    total = lax.dot_general(grads, rows_ref[...], over_voxels, preferred_element_type=F32)
    middle = 4 * width_out
    ones = jnp.ones((16, grads.shape[1]), BF16)
    bias = lax.dot_general(
        ones, grad_ref[middle : middle + width_out], over_voxels, preferred_element_type=F32
    )
    count = total.shape[0]
    rounded = total.astype(BF16)
    out_ref[:count] = rounded[:, : 2 * width_in]
    last = rounded[:, 2 * width_in :]
    out_ref[count : count + count // 2] = jnp.concatenate(
        [last[: count // 2], last[count // 2 :]], axis=1
    )
    high = bias.astype(BF16)
    rest = bias - high.astype(F32)
    mid = rest.astype(BF16)
    low = (rest - mid.astype(F32)).astype(BF16)
    row = lax.broadcasted_iota(jnp.int32, bias.shape, 0)
    nothing = jnp.zeros_like(bias)
    terms = jnp.where(
        row == 0,
        high.astype(F32),
        jnp.where(row == 1, mid.astype(F32), jnp.where(row == 2, low.astype(F32), nothing)),
    ).astype(BF16)
    out_ref[count + count // 2 :] = jnp.concatenate(
        [terms, jnp.zeros((16, LANES - width_out), BF16)], axis=1
    )


def finish_filter(own_ref, other_ref, weight_ref, bias_ref):
    _, width_out, width_in = weight_ref.shape
    count = 9 * width_out
    half = count // 2
    both = own_ref[...].astype(F32) + other_ref[...].astype(F32)
    for bc in range(9):
        rows = slice(bc * width_out, (bc + 1) * width_out)
        first = both[rows]
        weight_ref[bc] = first[:, :width_in]
        weight_ref[9 + bc] = first[:, width_in:]
        for step in range(0, width_out, 16):
            start = bc * width_out + step
            if start < half:
                piece = both[count + start : count + start + 16, :width_in]
            else:
                start -= half
                piece = both[count + start : count + start + 16, width_in:]
            weight_ref[18 + bc, step : step + 16] = piece
    first = count + half
    mine = own_ref[first:].astype(F32)
    theirs = other_ref[first:].astype(F32)
    bias_ref[...] = (
        jnp.sum(mine, axis=0, keepdims=True) + jnp.sum(theirs, axis=0, keepdims=True)
    )[:, :width_out]


def add_shares(shares_ref, out_ref):
    total = shares_ref[0].astype(F32)
    for k in range(1, shares_ref.shape[0]):
        total = total + shares_ref[k].astype(F32)
    out_ref[...] = total


def local(features, weight, bias_vector, cotangent):
    rows_y, width_in, _ = features.shape
    width_out = weight.shape[2]
    n_ci, n_co = lax.axis_size("ci"), lax.axis_size("co")
    shape = jax.ShapeDtypeStruct
    side = lax.axis_index("sp").astype(jnp.int32).reshape(1)
    swap = [(0, 1), (1, 0)]
    taps = weight.transpose(0, 2, 1)
    work = 2 * 27 * rows_y * LANES * width_in * width_out
    size = rows_y * LANES * 2

    edge = call(
        pack_features,
        shape((rows_y // 4, width_in, LANES), BF16),
        [SMEM, VMEM],
        0,
        2 * size * width_in,
    )(side, features)
    halo = lax.ppermute(edge, "sp", swap)
    partial = call(
        forward,
        shape((rows_y, width_out, LANES), BF16),
        [SMEM, VMEM, VMEM, VMEM],
        work,
        size * (width_in + width_out),
        [
            pltpu.VMEM((rows_y + 2, 3 * width_in, LANES), BF16),
            pltpu.VMEM((3 * width_out, 9 * width_in), BF16),
        ],
    )(side, features, halo, taps)
    shares = lax.all_to_all(
        partial.reshape(n_ci, rows_y // n_ci, width_out, LANES), "ci", 0, 0, tiled=True
    )
    block = (rows_y // n_ci, width_out, LANES)
    activated, grad_pre, edge = call(
        pointwise,
        (shape(block, BF16), shape(block, BF16), shape((width_out, LANES), BF16)),
        [SMEM, VMEM, VMEM, VMEM],
        0,
        2 * size * width_out,
    )(side, shares, bias_vector.reshape(width_out, 1), cotangent)
    halo = lax.ppermute(edge, "sp", swap)
    rows = 5 * width_out
    copies = call(
        replicate, shape((n_ci, rows, LANES), BF16), [VMEM, VMEM], 0, 2 * size * width_out
    )(grad_pre, halo)
    gathered = lax.all_to_all(copies, "ci", 0, 0, tiled=True)
    shares = call(
        backward,
        shape((rows_y, width_in, LANES), BF16),
        [SMEM, VMEM, VMEM],
        work,
        size * (width_in + width_out),
        [
            pltpu.VMEM((rows_y + 2, 3 * width_out, LANES), BF16),
            pltpu.VMEM((3 * width_in, 9 * width_out), BF16),
        ],
    )(side, gathered, taps)
    shares = lax.all_to_all(
        shares.reshape(n_co, rows_y // n_co, width_in, LANES), "co", 0, 0, tiled=True
    )
    packed = call(
        filter_gradient,
        shape((9 * width_out + 9 * width_out // 2 + 16, LANES), BF16),
        [SMEM, VMEM, VMEM],
        work,
        size * (width_in + width_out),
        [
            pltpu.VMEM((9 * width_out, rows_y * LANES), BF16),
            pltpu.VMEM((3 * width_in, rows_y * LANES), BF16),
        ],
    )(side, features, gathered)
    other = lax.ppermute(packed, "sp", swap)
    input_grad = call(
        add_shares,
        shape((rows_y // n_co, width_in, LANES), F32),
        [VMEM],
        0,
        size * width_in,
    )(shares)
    weight_grad, bias_grad = call(
        finish_filter,
        (shape((27, width_out, width_in), F32), shape((1, width_out), F32)),
        [VMEM, VMEM],
        0,
        27 * 4 * width_in * width_out,
    )(packed, other)
    return (activated, input_grad, weight_grad.transpose(0, 2, 1), bias_grad.reshape(width_out))


def solution(mesh):
    placed = (P(None, "ci", "sp"), P(None, "ci", "co"), P("co"), P("ci", "co", "sp"))
    return jax.shard_map(
        local,
        mesh=mesh,
        in_specs=placed,
        out_specs=(P("ci", "co", "sp"), P("co", "ci", "sp"), P(None, "ci", "co"), P("co")),
        check_vma=False,
    )
```

profile of v0, /device:TPU:1, one launch (start us, length us, event | category | flops | bytes accessed | tf_op | source)
XLA Modules:
  0.0 69.4 jit_solution(15945790347249405189)
XLA Ops:
  0.6 0.0 copy-start
  0.6 1.0 %copy-done = bf16[32,64,128]{2,1,0:T(8,128)(2,1)S(1)} copy-done((bf16[32,64,128]{2,1,0:T(8,128)(2,1)S(1)}, bf16[32,64,128]{2,1,0:T(8,128)(2,1)}, u32[]{:S(2)}) %copy-start) | copy-done | bytes 524312
  1.7 0.0 copy-start.3
  1.7 0.2 shard_map.75
  1.9 2.1 %collective-permute-start = (bf16[8,64,128]{2,1,0:T(8,128)(2,1)S(1)}, bf16[8,64,128]{2,1,0:T(8,128)(2,1)S(1)}, u32[]{:S(2)}, u32[]{:S(2)}) collective-permute-start(bf16[8,64,128]{2,1,0:T(8,128)(2,1)S(1)} %shard_map.75), channel_id=1, source_target_pairs={{0,1},{1,0},{2,3},{3,2},{4,5},{5,4},{6,7},{7,6},{8,9},{9,8},{10,11... | collective-permute-start | bytes 393224 | tf_op jit(solution)/shard_map/ppermute | solution.py:280
  4.0 2.4 %collective-permute-done.halo_ref = bf16[8,64,128]{2,1,0:T(8,128)(2,1)S(1)} collective-permute-done((bf16[8,64,128]{2,1,0:T(8,128)(2,1)S(1)}, bf16[8,64,128]{2,1,0:T(8,128)(2,1)S(1)}, u32[]{:S(2)}, u32[]{:S(2)}) %collective-permute-start) | collective-permute-done | bytes 131104 | tf_op jit(solution)/shard_map/ppermute | solution.py:280
  6.4 0.0 copy-done.3
  6.4 2.0 %shard_map.76 = bf16[32,32,128]{2,1,0:T(8,128)(2,1)} custom-call(s32[1]{0:T(128)} %bitcast.side_ref, bf16[32,64,128]{2,1,0:T(8,128)(2,1)S(1)} %copy-done, bf16[8,64,128]{2,1,0:T(8,128)(2,1)S(1)} %collective-permute-done.halo_ref, bf16[27,32,64]{2,1,0:T(8,128)(2,1)S(1)} %bitcast.7), custom_call_target="tpu_custom_call" | custom-call | flops 452984832 | bytes 786432 | tf_op jit(solution)/shard_map/pallas_call | solution.py:281
  8.4 0.0 copy-start.2
  8.4 9.1 %all-to-all-start = ((bf16[8,4,32,128]{3,2,1,0:T(8,128)(2,1)}), bf16[8,4,32,128]{3,2,1,0:T(8,128)(2,1)S(1)}, u32[]{:S(2)}, u32[]{:S(2)}) async-start(bf16[8,4,32,128]{3,2,1,0:T(8,128)(2,1)} %bitcast.2), calls=%async_computation | async-start | bytes 524288 | tf_op jit(solution)/shard_map/all_to_all | solution.py:292
  17.5 0.0 copy-start.4
  17.5 0.7 copy-done.4
  18.1 0.1 copy.8.bias_ref
  18.2 8.6 %all-to-all-done.partial_ref = bf16[8,4,32,128]{3,2,1,0:T(8,128)(2,1)S(1)} async-done(((bf16[8,4,32,128]{3,2,1,0:T(8,128)(2,1)}), bf16[8,4,32,128]{3,2,1,0:T(8,128)(2,1)S(1)}, u32[]{:S(2)}, u32[]{:S(2)}) %all-to-all-start) | async-done | bytes 262176 | tf_op jit(solution)/shard_map/all_to_all | solution.py:292
  26.8 0.0 copy-done.2
  26.8 0.7 %shard_map.77 = (bf16[4,32,128]{2,1,0:T(8,128)(2,1)}, bf16[4,32,128]{2,1,0:T(8,128)(2,1)S(1)}, bf16[32,128]{1,0:T(8,128)(2,1)S(1)}) custom-call(s32[1]{0:T(128)} %bitcast.side_ref, bf16[8,4,32,128]{3,2,1,0:T(8,128)(2,1)S(1)} %all-to-all-done.partial_ref, f32[32,1]{1,0:T(8,128)S(1)} %copy.8.bias_ref, bf16[4,32,128]{2,1,0:T(8,128)(2,1)S(1)} %copy-done.2), custom_call_target="tpu_custom_call" | custom-call | bytes 524288 | tf_op jit(solution)/shard_map/pallas_call | solution.py:296
  27.5 1.2 %collective-permute-start.1 = (bf16[32,128]{1,0:T(8,128)(2,1)S(1)}, bf16[32,128]{1,0:T(8,128)(2,1)S(1)}, u32[]{:S(2)}, u32[]{:S(2)}) collective-permute-start(bf16[32,128]{1,0:T(8,128)(2,1)S(1)} %get-tuple-element.11), channel_id=1, source_target_pairs={{0,1},{1,0},{2,3},{3,2},{4,5},{5,4},{6,7},{7,6},{8,9},{9,8},{10,11... | collective-permute-start | bytes 24584 | tf_op jit(solution)/shard_map/ppermute | solution.py:303
  28.7 1.3 %collective-permute-done.1.halo_ref = bf16[32,128]{1,0:T(8,128)(2,1)S(1)} collective-permute-done((bf16[32,128]{1,0:T(8,128)(2,1)S(1)}, bf16[32,128]{1,0:T(8,128)(2,1)S(1)}, u32[]{:S(2)}, u32[]{:S(2)}) %collective-permute-start.1) | collective-permute-done | bytes 8224 | tf_op jit(solution)/shard_map/ppermute | solution.py:303
  30.1 13.2 %all_to_all.15.gathered_ref = bf16[8,160,128]{2,1,0:T(8,128)(2,1)S(1)} all-to-all(bf16[8,160,128]{2,1,0:T(8,128)(2,1)S(1)} %shard_map.78), channel_id=1, replica_groups=mesh['ci'=8,'co'=16,'sp'=2] {'ci'}, dimensions={0} | all-to-all | bytes 655360 | tf_op jit(solution)/shard_map/all_to_all | solution.py:308
  43.3 2.0 %shard_map.79 = bf16[32,64,128]{2,1,0:T(8,128)(2,1)} custom-call(s32[1]{0:T(128)} %bitcast.side_ref, bf16[8,160,128]{2,1,0:T(8,128)(2,1)S(1)} %all_to_all.15.gathered_ref, bf16[27,32,64]{2,1,0:T(8,128)(2,1)S(1)} %bitcast.8), custom_call_target="tpu_custom_call" | custom-call | flops 452984832 | bytes 786432 | tf_op jit(solution)/shard_map/pallas_call | solution.py:309
  45.3 0.0 copy-start.1
  45.3 12.1 %all-to-all-start.2 = ((bf16[16,2,64,128]{3,2,1,0:T(8,128)(2,1)}), bf16[16,2,64,128]{3,2,1,0:T(8,128)(2,1)S(1)}, u32[]{:S(2)}, u32[]{:S(2)}) async-start(bf16[16,2,64,128]{3,2,1,0:T(8,128)(2,1)} %bitcast.4), calls=%async_computation.2 | async-start | bytes 1048576 | tf_op jit(solution)/shard_map/all_to_all | solution.py:320
  57.4 0.0 copy-done.1
  57.4 1.9 %shard_map.81.own_ref = bf16[448,128]{1,0:T(8,128)(2,1)S(1)} custom-call(s32[1]{0:T(128)} %bitcast.side_ref, bf16[32,64,128]{2,1,0:T(8,128)(2,1)S(1)} %copy-done.1, bf16[8,160,128]{2,1,0:T(8,128)(2,1)S(1)} %all_to_all.15.gathered_ref), custom_call_target="tpu_custom_call" | custom-call | flops 452984832 | bytes 786432 | tf_op jit(solution)/shard_map/pallas_call | solution.py:323
  59.3 0.4 collective-permute-start.2
  59.7 7.3 %collective-permute-done.2.other_ref = bf16[448,128]{1,0:T(8,128)(2,1)S(1)} collective-permute-done((bf16[448,128]{1,0:T(8,128)(2,1)S(1)}, bf16[448,128]{1,0:T(8,128)(2,1)S(1)}, u32[]{:S(2)}, u32[]{:S(2)}) %collective-permute-start.2) | collective-permute-done | bytes 114720 | tf_op jit(solution)/shard_map/ppermute | solution.py:334
  67.1 0.9 %shard_map.82 = (f32[27,32,64]{2,1,0:T(8,128)}, f32[1,32]{1,0:T(1,128)}) custom-call(bf16[448,128]{1,0:T(8,128)(2,1)S(1)} %shard_map.81.own_ref, bf16[448,128]{1,0:T(8,128)(2,1)S(1)} %collective-permute-done.2.other_ref), custom_call_target="tpu_custom_call" | custom-call | bytes 221184 | tf_op jit(solution)/shard_map/pallas_call | solution.py:342
  67.9 0.7 %all-to-all-done.2.shares_ref = bf16[16,2,64,128]{3,2,1,0:T(8,128)(2,1)S(1)} async-done(((bf16[16,2,64,128]{3,2,1,0:T(8,128)(2,1)}), bf16[16,2,64,128]{3,2,1,0:T(8,128)(2,1)S(1)}, u32[]{:S(2)}, u32[]{:S(2)}) %all-to-all-start.2) | async-done | bytes 524320 | tf_op jit(solution)/shard_map/all_to_all | solution.py:320
  68.7 0.7 %shard_map.80 = f32[2,64,128]{2,1,0:T(8,128)} custom-call(bf16[16,2,64,128]{3,2,1,0:T(8,128)(2,1)S(1)} %all-to-all-done.2.shares_ref), custom_call_target="tpu_custom_call" | custom-call | bytes 524288 | tf_op jit(solution)/shard_map/pallas_call | solution.py:335
  (1 shorter events, 0.0 us)
Async XLA Ops:
  0.6 1.0 %copy-start = (bf16[32,64,128]{2,1,0:T(8,128)(2,1)S(1)}, bf16[32,64,128]{2,1,0:T(8,128)(2,1)}, u32[]{:S(2)}) copy-start(bf16[32,64,128]{2,1,0:T(8,128)(2,1)} %features_ref.5) | copy-start | bytes 1572868
  1.7 4.7 %copy-start.3 = (bf16[27,64,32]{1,2,0:T(8,128)(2,1)S(1)}, bf16[27,64,32]{1,2,0:T(8,128)(2,1)}, u32[]{:S(2)}) copy-start(bf16[27,64,32]{1,2,0:T(8,128)(2,1)} %param.5) | copy-start | bytes 331780
  1.9 4.5 %collective-permute-start = (bf16[8,64,128]{2,1,0:T(8,128)(2,1)S(1)}, bf16[8,64,128]{2,1,0:T(8,128)(2,1)S(1)}, u32[]{:S(2)}, u32[]{:S(2)}) collective-permute-start(bf16[8,64,128]{2,1,0:T(8,128)(2,1)S(1)} %shard_map.75), channel_id=1, source_target_pairs={{0,1},{1,0},{2,3},{3,2},{4,5},{5,4},{6,7},{7,6},{8,9},{9,8},{10,11... | collective-permute-start | bytes 393224 | tf_op jit(solution)/shard_map/ppermute | solution.py:280
  8.4 18.4 %copy-start.2 = (bf16[4,32,128]{2,1,0:T(8,128)(2,1)S(1)}, bf16[4,32,128]{2,1,0:T(8,128)(2,1)}, u32[]{:S(2)}) copy-start(bf16[4,32,128]{2,1,0:T(8,128)(2,1)} %cotangent_ref.1) | copy-start | bytes 98308
  8.4 18.4 %all-to-all-start = ((bf16[8,4,32,128]{3,2,1,0:T(8,128)(2,1)}), bf16[8,4,32,128]{3,2,1,0:T(8,128)(2,1)S(1)}, u32[]{:S(2)}, u32[]{:S(2)}) async-start(bf16[8,4,32,128]{3,2,1,0:T(8,128)(2,1)} %bitcast.2), calls=%async_computation | async-start | bytes 524288 | tf_op jit(solution)/shard_map/all_to_all | solution.py:292
  17.5 0.7 copy-start.4
  27.5 2.5 %collective-permute-start.1 = (bf16[32,128]{1,0:T(8,128)(2,1)S(1)}, bf16[32,128]{1,0:T(8,128)(2,1)S(1)}, u32[]{:S(2)}, u32[]{:S(2)}) collective-permute-start(bf16[32,128]{1,0:T(8,128)(2,1)S(1)} %get-tuple-element.11), channel_id=1, source_target_pairs={{0,1},{1,0},{2,3},{3,2},{4,5},{5,4},{6,7},{7,6},{8,9},{9,8},{10,11... | collective-permute-start | bytes 24584 | tf_op jit(solution)/shard_map/ppermute | solution.py:303
  45.3 12.1 %copy-start.1 = (bf16[32,64,128]{2,1,0:T(8,128)(2,1)S(1)}, bf16[32,64,128]{2,1,0:T(8,128)(2,1)}, u32[]{:S(2)}) copy-start(bf16[32,64,128]{2,1,0:T(8,128)(2,1)} %features_ref.5) | copy-start | bytes 1572868
  45.3 23.4 %all-to-all-start.2 = ((bf16[16,2,64,128]{3,2,1,0:T(8,128)(2,1)}), bf16[16,2,64,128]{3,2,1,0:T(8,128)(2,1)S(1)}, u32[]{:S(2)}, u32[]{:S(2)}) async-start(bf16[16,2,64,128]{3,2,1,0:T(8,128)(2,1)} %bitcast.4), calls=%async_computation.2 | async-start | bytes 1048576 | tf_op jit(solution)/shard_map/all_to_all | solution.py:320
  59.3 7.8 %collective-permute-start.2 = (bf16[448,128]{1,0:T(8,128)(2,1)S(1)}, bf16[448,128]{1,0:T(8,128)(2,1)S(1)}, u32[]{:S(2)}, u32[]{:S(2)}) collective-permute-start(bf16[448,128]{1,0:T(8,128)(2,1)S(1)} %shard_map.81.own_ref), channel_id=1, source_target_pairs={{0,1},{1,0},{2,3},{3,2},{4,5},{5,4},{6,7},{7,6},{8,9},{9,8},{10,11... | collective-permute-start | bytes 344072 | tf_op jit(solution)/shard_map/ppermute | solution.py:334
where the time goes:
time: 69.8 us; the launch traced here: 69.4 us
  starting transfers between devices  25 us (36%)
  waiting for transfers between devices  20.3 us (29%)
  blocking collectives  13.2 us (19%)
  Pallas kernels  8.45 us (12%)
  local copies, waits for them, and re-layouts  1.79 us (3%)
    all_to_all x1, blocking collectives, local(): gathered = lax.all_to_all(copies, 'ci', 0, 0, tiled=True)  13.2 us
    all_to_all x1, starting transfers between devices, local(): lax.all_to_all(shares.reshape(n_co, rows_y // n_co, width_in, LANES), 'co...  12.1 us
    all_to_all x1, starting transfers between devices, local(): lax.all_to_all(partial.reshape(n_ci, rows_y // n_ci, width_out, LANES), '...  9.11 us
    all_to_all x1, waiting for transfers between devices, local(): lax.all_to_all(partial.reshape(n_ci, rows_y // n_ci, width_out, LANES), '...  8.57 us
    ppermute x1, waiting for transfers between devices, local(): other = lax.ppermute(packed, 'sp', swap)  7.33 us
    ppermute x2, waiting for transfers between devices, local(): halo = lax.ppermute(edge, 'sp', swap)  3.63 us
    ppermute x2, starting transfers between devices, local(): halo = lax.ppermute(edge, 'sp', swap)  3.35 us
    pallas_call x1, Pallas kernels, local(): call(backward, shape((rows_y, width_in, LANES), BF16), [SMEM, VMEM, VMEM]...  2.02 us
  transfers between devices with their start and end apart: 5, of which 5 were waited for; matrix products, arithmetic and copies ran while one was open for 0% of the time, Pallas kernels for 4%

commit v1 on v0

--- a/solution.py
+++ b/solution.py
@@ -11,6 +11,7 @@
 F32 = jnp.float32
 VMEM = pl.BlockSpec(memory_space=pltpu.VMEM)
 SMEM = pl.BlockSpec(memory_space=pltpu.SMEM)
+HBM = pl.BlockSpec(memory_space=pltpu.HBM)
 
 
 def call(body, outs, specs, flops, moved, scratch=()):
@@ -38,14 +39,13 @@
     return packed
 
 
-def neighbours(own, low, high, k):
+def neighbours(own, low=None, high=None, k=0):
     at = lane(own.shape)
-    before = jnp.where(at < SZ, pltpu.roll(low, (-SZ * k) % LANES, 1), pltpu.roll(own, SZ, 1))
-    after = jnp.where(
-        at >= LANES - SZ,
-        pltpu.roll(high, (LANES - SZ - SZ * k) % LANES, 1),
-        pltpu.roll(own, LANES - SZ, 1),
-    )
+    zero = jnp.zeros_like(own)
+    left = zero if low is None else pltpu.roll(low, (-SZ * k) % LANES, 1)
+    right = zero if high is None else pltpu.roll(high, (LANES - SZ - SZ * k) % LANES, 1)
+    before = jnp.where(at < SZ, left, pltpu.roll(own, SZ, 1))
+    after = jnp.where(at >= LANES - SZ, right, pltpu.roll(own, LANES - SZ, 1))
     return before, own, after
 
 
@@ -69,72 +69,130 @@
     return parts
 
 
-def pack_features(side_ref, features_ref, out_ref):
-    side = side_ref[0]
-    for group in range(out_ref.shape[0]):
-        out_ref[group] = pack_plane(side, [features_ref[4 * group + k] for k in range(4)])
-
-
-def correlate(taps_ref, spread_ref, rows_y, width, store):
+def correlate_rows(taps, spread_ref, y, width, store):
     depth = 3 * spread_ref.shape[1]
-    taps = taps_ref[...]
-    for y in range(0, rows_y, 2):
-        columns = jnp.concatenate(
-            [spread_ref[y + k : y + k + 3].reshape(depth, LANES) for k in range(2)], axis=1
-        )
-        product = jnp.dot(taps, columns, preferred_element_type=F32)
-        parts = along_z([product[c * width : (c + 1) * width] for c in range(3)])
-        for k in range(2):
-            store(y + k, parts[k].astype(BF16))
-
-
-def forward(side_ref, features_ref, halo_ref, weight_ref, out_ref, spread_ref, taps_ref):
+    columns = jnp.concatenate(
+        [spread_ref[y + k : y + k + 3].reshape(depth, LANES) for k in range(2)], axis=1
+    )
+    product = jnp.dot(taps, columns, preferred_element_type=F32)
+    parts = along_z([product[c * width : (c + 1) * width] for c in range(3)])
+    for k in range(2):
+        store(y + k, parts[k].astype(BF16))
+
+
+def forward(
+    side_ref, features_hbm, weight_hbm, out_ref,
+    features_ref, weight_ref, spread_ref, taps_ref, edge_taps_ref, edge_ref, sems,
+):
     rows_y, width_in, _ = features_ref.shape
     width_out = weight_ref.shape[1]
+    groups = rows_y // 4
+    pieces = sems.shape[0] - 1
+    step = rows_y // pieces
+    fetch = [
+        pltpu.make_async_copy(
+            features_hbm.at[pl.ds(k * step, step)], features_ref.at[pl.ds(k * step, step)], sems.at[k]
+        )
+        for k in range(pieces)
+    ]
+    fetch_weight = pltpu.make_async_copy(weight_hbm, weight_ref, sems.at[pieces])
+    fetch[0].start()
+    fetch_weight.start()
+    for copy in fetch[1:]:
+        copy.start()
     side = side_ref[0]
     blank = jnp.zeros(spread_ref.shape[1:], BF16)
     spread_ref[0] = blank
     spread_ref[rows_y + 1] = blank
-    for group in range(rows_y // 4):
-        low, high = split_halo(side, halo_ref[group])
+    fetch_weight.wait()
+    for c in range(3):
+        rows = slice(c * width_out, (c + 1) * width_out)
+        taps_ref[rows] = jnp.concatenate([weight_ref[3 * ab + c] for ab in range(9)], axis=1)
+        edge_taps_ref[rows] = jnp.concatenate(
+            [weight_ref[9 * a + c + 6 * side] for a in range(3)], axis=1
+        )
+    taps = taps_ref[...]
+
+    def store(y, value):
+        start = y % 4 * width_out
+        out_ref[y // 4, start : start + width_out] = value
+
+    done = 0
+    for group in range(groups):
+        if group * 4 % step == 0:
+            fetch[group * 4 // step].wait()
+        planes = [features_ref[4 * group + k] for k in range(4)]
         for k in range(4):
-            y = 4 * group + k
-            seen = neighbours(features_ref[y], low, high, k)
+            seen = neighbours(planes[k])
             for b in range(3):
-                spread_ref[y + 1, b * width_in : (b + 1) * width_in] = seen[b]
-    for c in range(3):
-        taps_ref[c * width_out : (c + 1) * width_out] = jnp.concatenate(
-            [weight_ref[3 * ab + c] for ab in range(9)], axis=1
+                spread_ref[4 * group + k + 1, b * width_in : (b + 1) * width_in] = seen[b]
+        edge_ref[group + 1] = pack_plane(side, planes)
+        while done + 2 < 4 * group + 4 or (group == groups - 1 and done < rows_y):
+            correlate_rows(taps, spread_ref, done, width_out, store)
+            done += 2
+    none = jnp.zeros(edge_ref.shape[1:], BF16)
+    edge_ref[0] = none
+    edge_ref[groups + 1] = none
+    at = lane((width_in, LANES))
+    columns = []
+    for group in range(groups):
+        last, here, following = (edge_ref[group + k] for k in range(3))
+        above = jnp.where(at < SZ, pltpu.roll(last, SZ, 1), pltpu.roll(here, SZ, 1))
+        below = jnp.where(
+            at >= LANES - SZ,
+            pltpu.roll(following, LANES - SZ, 1),
+            pltpu.roll(here, LANES - SZ, 1),
         )
-
-    def store(y, value):
-        out_ref[y] = value
-
-    correlate(taps_ref, spread_ref, rows_y, width_out, store)
-
-
-def pointwise(side_ref, partial_ref, bias_ref, cotangent_ref, act_ref, grad_ref, edge_ref):
-    total = partial_ref[0].astype(F32)
-    for k in range(1, partial_ref.shape[0]):
-        total = total + partial_ref[k].astype(F32)
-    pre = total + bias_ref[...][None]
+        columns.append(jnp.concatenate([above, here, below], axis=0))
+    product = jnp.dot(
+        edge_taps_ref[...], jnp.concatenate(columns, axis=1), preferred_element_type=F32
+    )
+    parts = along_z([product[c * width_out : (c + 1) * width_out] for c in range(3)])
+    for group in range(groups):
+        out_ref[group, 4 * width_out :] = parts[group].astype(BF16)
+
+
+def reduce_rows(side_ref, shares_ref, cotangent_ref, own_ref, message_ref):
+    total = shares_ref[0].astype(F32)
+    for k in range(1, shares_ref.shape[0]):
+        total = total + shares_ref[k].astype(F32)
+    rows, width, _ = cotangent_ref.shape
+    planes = [total[k * width : (k + 1) * width] for k in range(rows)]
+    for k in range(rows):
+        own_ref[k] = planes[k]
+    side = side_ref[0]
+    message_ref[0] = total[rows * width :]
+    message_ref[1] = pack_plane(side, planes)
+    message_ref[2] = pack_plane(side, [cotangent_ref[k].astype(F32) for k in range(rows)])
+
+
+def gelu(pre, cotangent):
     scale, cubic = 0.7978845608, 0.044715
     square = pre * pre
     bend = jnp.tanh(scale * (pre + cubic * (square * pre)))
     half = 0.5 * (1.0 + bend)
-    act_ref[...] = (pre * half).astype(BF16)
     slope = half + 0.5 * pre * (1.0 - bend * bend) * (scale * (1.0 + 3.0 * cubic * square))
-    grad = (cotangent_ref[...].astype(F32) * slope).astype(BF16)
-    grad_ref[...] = grad
-    edge_ref[...] = pack_plane(side_ref[0], [grad[k] for k in range(4)])
-
-
-def replicate(grad_ref, halo_ref, out_ref):
-    rows = grad_ref.shape[0] * grad_ref.shape[1]
-    own = grad_ref[...].reshape(rows, LANES)
+    return (pre * half).astype(BF16), (cotangent * slope).astype(BF16)
+
+
+def pointwise(side_ref, own_ref, mine_ref, theirs_ref, bias_ref, cotangent_ref, act_ref, out_ref):
+    rows, width, _ = own_ref.shape
+    side = side_ref[0]
+    bias = jnp.broadcast_to(bias_ref[...], (width, LANES))
+    at = lane((width, LANES))
+    edge = at // SZ == 3 * (1 - side)
+    added = theirs_ref[0]
+    grads = []
+    for k in range(rows):
+        moved = pltpu.roll(added, lax.rem(3 * SZ * (1 - side) - SZ * k + LANES, LANES), 1)
+        pre = own_ref[k] + jnp.where(edge, moved, 0.0) + bias
+        act, grad = gelu(pre, cotangent_ref[k].astype(F32))
+        act_ref[k] = act
+        grads.append(grad)
+    _, grad = gelu(theirs_ref[1] + mine_ref[0] + bias, theirs_ref[2])
+    block = jnp.concatenate(grads + [grad], axis=0)
     for k in range(out_ref.shape[0]):
-        out_ref[k, :rows] = own
-        out_ref[k, rows:] = halo_ref[...]
+        out_ref[k] = block
 
 
 def spread_gradient(side, gathered_ref, width, put):
@@ -165,7 +223,9 @@
     def store(y, value):
         out_ref[y] = value
 
-    correlate(taps_ref, spread_ref, rows_y, width_in, store)
+    taps = taps_ref[...]
+    for y in range(0, rows_y, 2):
+        correlate_rows(taps, spread_ref, y, width_in, store)
 
 
 def filter_gradient(side_ref, features_ref, gathered_ref, out_ref, grad_ref, rows_ref):
@@ -270,42 +330,53 @@
     work = 2 * 27 * rows_y * LANES * width_in * width_out
     size = rows_y * LANES * 2
 
-    edge = call(
-        pack_features,
-        shape((rows_y // 4, width_in, LANES), BF16),
-        [SMEM, VMEM],
-        0,
-        2 * size * width_in,
-    )(side, features)
-    halo = lax.ppermute(edge, "sp", swap)
+    block = 5 * width_out
     partial = call(
         forward,
-        shape((rows_y, width_out, LANES), BF16),
-        [SMEM, VMEM, VMEM, VMEM],
+        shape((n_ci, block, LANES), BF16),
+        [SMEM, HBM, HBM],
         work,
         size * (width_in + width_out),
         [
+            pltpu.VMEM(features.shape, BF16),
+            pltpu.VMEM(taps.shape, BF16),
             pltpu.VMEM((rows_y + 2, 3 * width_in, LANES), BF16),
             pltpu.VMEM((3 * width_out, 9 * width_in), BF16),
+            pltpu.VMEM((3 * width_out, 3 * width_in), BF16),
+            pltpu.VMEM((rows_y // 4 + 2, width_in, LANES), BF16),
+            pltpu.SemaphoreType.DMA((5,)),
         ],
-    )(side, features, halo, taps)
-    shares = lax.all_to_all(
-        partial.reshape(n_ci, rows_y // n_ci, width_out, LANES), "ci", 0, 0, tiled=True
-    )
-    block = (rows_y // n_ci, width_out, LANES)
-    activated, grad_pre, edge = call(
-        pointwise,
-        (shape(block, BF16), shape(block, BF16), shape((width_out, LANES), BF16)),
-        [SMEM, VMEM, VMEM, VMEM],
+    )(side, features, taps)
+    shares = lax.all_to_all(partial, "ci", 0, 0, tiled=True)
+    own, mine = call(
+        reduce_rows,
+        (shape(cotangent.shape, F32), shape((3, width_out, LANES), F32)),
+        [SMEM, VMEM, VMEM],
         0,
         2 * size * width_out,
-    )(side, shares, bias_vector.reshape(width_out, 1), cotangent)
-    halo = lax.ppermute(edge, "sp", swap)
-    rows = 5 * width_out
-    copies = call(
-        replicate, shape((n_ci, rows, LANES), BF16), [VMEM, VMEM], 0, 2 * size * width_out
-    )(grad_pre, halo)
+    )(side, shares, cotangent)
+    theirs = lax.ppermute(mine, "sp", swap)
+    activated, copies = call(
+        pointwise,
+        (shape(cotangent.shape, BF16), shape((n_ci, block, LANES), BF16)),
+        [SMEM, VMEM, VMEM, VMEM, VMEM, VMEM],
+        0,
+        2 * size * width_out,
+    )(side, own, mine, theirs, bias_vector.reshape(width_out, 1), cotangent)
     gathered = lax.all_to_all(copies, "ci", 0, 0, tiled=True)
+    packed = call(
+        filter_gradient,
+        shape((9 * width_out + 9 * width_out // 2 + 16, LANES), BF16),
+        [SMEM, VMEM, VMEM],
+        work,
+        size * (width_in + width_out),
+        [
+            pltpu.VMEM((9 * width_out, rows_y * LANES), BF16),
+            pltpu.VMEM((3 * width_in, rows_y * LANES), BF16),
+        ],
+    )(side, features, gathered)
+    other = lax.ppermute(packed, "sp", swap)
+    gathered, packed = lax.optimization_barrier((gathered, packed))
     shares = call(
         backward,
         shape((rows_y, width_in, LANES), BF16),
@@ -320,18 +391,6 @@
     shares = lax.all_to_all(
         shares.reshape(n_co, rows_y // n_co, width_in, LANES), "co", 0, 0, tiled=True
     )
-    packed = call(
-        filter_gradient,
-        shape((9 * width_out + 9 * width_out // 2 + 16, LANES), BF16),
-        [SMEM, VMEM, VMEM],
-        work,
-        size * (width_in + width_out),
-        [
-            pltpu.VMEM((9 * width_out, rows_y * LANES), BF16),
-            pltpu.VMEM((3 * width_in, rows_y * LANES), BF16),
-        ],
-    )(side, features, gathered)
-    other = lax.ppermute(packed, "sp", swap)
     input_grad = call(
         add_shares,
         shape((rows_y // n_co, width_in, LANES), F32),

time: 69.8 us -> 70.7 us (1.013)
  blocking collectives: 13.2 us -> 33.4 us
  starting transfers between devices: 25 us -> 12.9 us
  waiting for transfers between devices: 20.3 us -> 11.7 us
  Pallas kernels: 8.45 us -> 9.56 us
    all_to_all x0 -> x1, blocking collectives: none -> 20.5 us  [local(): shares = lax.all_to_all(partial, 'ci', 0, 0, tiled=True)]
    all_to_all x1 -> x0, starting transfers between devices: 9.11 us -> none  [local(): lax.all_to_all(partial.reshape(n_ci, rows_y // n_ci, width_out, LANES), '...]
    all_to_all x1 -> x0, waiting for transfers between devices: 8.57 us -> none  [local(): lax.all_to_all(partial.reshape(n_ci, rows_y // n_ci, width_out, LANES), '...]
    ppermute x2 -> x1, starting transfers between devices: 3.35 us -> 1.3 us  [local(): theirs = lax.ppermute(mine, 'sp', swap)]
    ppermute x2 -> x1, waiting for transfers between devices: 3.63 us -> 1.64 us  [local(): theirs = lax.ppermute(mine, 'sp', swap)]
    ppermute x1, waiting for transfers between devices: 7.33 us -> 9.33 us  [local(): other = lax.ppermute(packed, 'sp', swap)]
    pallas_call x4 -> x3, Pallas kernels: 2.96 us -> 4.04 us  [the longest x1 3.17 us: local(): call(forward, shape((n_ci, block, LANES), BF16), [SMEM, HBM, HBM], work,...]
    all_to_all x1, starting transfers between devices: 12.1 us -> 11.3 us  [local(): lax.all_to_all(shares.reshape(n_co, rows_y // n_co, width_in, LANES), 'co...]
  transfers between devices with their start and end apart: 5 -> 3, of which waited for: 5 -> 3; matrix products, arithmetic and copies ran while one was open for 0% -> 0% of each run, Pallas kernels for 4% -> 1%
where the time goes in v1:
time: 70.7 us; the launch traced here: 70.3 us
  blocking collectives  33.4 us (47%)
  starting transfers between devices  12.9 us (18%)
  waiting for transfers between devices  11.7 us (17%)
  Pallas kernels  9.56 us (14%)
  local copies, waits for them, and re-layouts  2.08 us (3%)
    all_to_all x1, blocking collectives, local(): shares = lax.all_to_all(partial, 'ci', 0, 0, tiled=True)  20.5 us
    all_to_all x1, blocking collectives, local(): gathered = lax.all_to_all(copies, 'ci', 0, 0, tiled=True)  12.9 us
    all_to_all x1, starting transfers between devices, local(): lax.all_to_all(shares.reshape(n_co, rows_y // n_co, width_in, LANES), 'co...  11.3 us
    ppermute x1, waiting for transfers between devices, local(): other = lax.ppermute(packed, 'sp', swap)  9.33 us
    pallas_call x1, Pallas kernels, local(): call(forward, shape((n_ci, block, LANES), BF16), [SMEM, HBM, HBM], work,...  3.17 us
    pallas_call x1, Pallas kernels, local(): call(backward, shape((rows_y, width_in, LANES), BF16), [SMEM, VMEM, VMEM]...  2.05 us
    unnamed x12, local copies, waits for them, and re-layouts  1.99 us
    pallas_call x1, Pallas kernels, local(): call(filter_gradient, shape((9 * width_out + 9 * width_out // 2 + 16, LAN...  1.88 us
  transfers between devices with their start and end apart: 3, of which 3 were waited for; matrix products, arithmetic and copies ran while one was open for 0% of the time, Pallas kernels for 1%

profile of v1, /device:TPU:1, one launch (start us, length us, event | category | flops | bytes accessed | tf_op | source)
XLA Modules:
  0.0 70.3 jit_solution(12914389236502676845)
XLA Ops:
  0.6 0.0 copy-start.1
  0.6 1.0 %copy-done.1 = bf16[32,64,128]{2,1,0:T(8,128)(2,1)S(1)} copy-done((bf16[32,64,128]{2,1,0:T(8,128)(2,1)S(1)}, bf16[32,64,128]{2,1,0:T(8,128)(2,1)}, u32[]{:S(2)}) %copy-start.1) | copy-done | bytes 524312
  1.7 0.0 copy-start.3
  1.7 0.9 %copy-done.3 = bf16[27,64,32]{1,2,0:T(8,128)(2,1)S(1)} copy-done((bf16[27,64,32]{1,2,0:T(8,128)(2,1)S(1)}, bf16[27,64,32]{1,2,0:T(8,128)(2,1)}, u32[]{:S(2)}) %copy-start.3) | copy-done | bytes 110616
  2.6 3.2 %shard_map.75 = bf16[8,160,128]{2,1,0:T(8,128)(2,1)S(1)} custom-call(s32[1]{0:T(128)} %bitcast.side_ref, bf16[32,64,128]{2,1,0:T(8,128)(2,1)S(1)} %copy-done.1, bf16[27,32,64]{2,1,0:T(8,128)(2,1)S(1)} %bitcast.6), custom_call_target="tpu_custom_call" | custom-call | flops 452984832 | bytes 786432 | tf_op jit(solution)/shard_map/pallas_call | solution.py:334
  5.8 0.0 copy-start
  5.8 20.5 %all_to_all.15.shares_ref = bf16[8,160,128]{2,1,0:T(8,128)(2,1)S(1)} all-to-all(bf16[8,160,128]{2,1,0:T(8,128)(2,1)S(1)} %shard_map.75), channel_id=1, replica_groups=mesh['ci'=8,'co'=16,'sp'=2] {'ci'}, dimensions={0} | all-to-all | bytes 655360 | tf_op jit(solution)/shard_map/all_to_all | solution.py:350
  26.3 0.0 copy-done
  26.3 0.0 copy-start.5
  26.3 0.1 shard_map.76
  26.4 0.0 copy-start.2
  26.4 1.3 %collective-permute-start = (f32[3,32,128]{2,1,0:T(8,128)S(1)}, f32[3,32,128]{2,1,0:T(8,128)S(1)}, u32[]{:S(2)}, u32[]{:S(2)}) collective-permute-start(f32[3,32,128]{2,1,0:T(8,128)S(1)} %get-tuple-element.13.mine_ref), channel_id=1, source_target_pairs={{0,1},{1,0},{2,3},{3,2},{4,5},{5,4},{6,7},{7,6},{8,9},{9,8},{10,11... | collective-permute-start | bytes 147464 | tf_op jit(solution)/shard_map/ppermute | solution.py:358
  27.7 0.0 copy-done.5
  27.7 0.1 copy.8.bias_ref
  27.8 1.6 %collective-permute-done.theirs_ref = f32[3,32,128]{2,1,0:T(8,128)S(1)} collective-permute-done((f32[3,32,128]{2,1,0:T(8,128)S(1)}, f32[3,32,128]{2,1,0:T(8,128)S(1)}, u32[]{:S(2)}, u32[]{:S(2)}) %collective-permute-start) | collective-permute-done | bytes 49184 | tf_op jit(solution)/shard_map/ppermute | solution.py:358
  29.5 0.8 %shard_map.77 = (bf16[4,32,128]{2,1,0:T(8,128)(2,1)}, bf16[8,160,128]{2,1,0:T(8,128)(2,1)S(1)}) custom-call(s32[1]{0:T(128)} %bitcast.side_ref, f32[4,32,128]{2,1,0:T(8,128)S(1)} %get-tuple-element.12.own_ref, f32[3,32,128]{2,1,0:T(8,128)S(1)} %get-tuple-element.13.mine_ref, f32[3,32,128]{2,1,0:T(8,128)S(1)} %collective-permute-done.theirs_ref, ...), custom_call_target="tpu_custom_call" | custom-call | bytes 524288 | tf_op jit(solution)/shard_map/pallas_call | solution.py:359
  30.2 12.9 %all_to_all.16.gathered_ref = bf16[8,160,128]{2,1,0:T(8,128)(2,1)S(1)} all-to-all(bf16[8,160,128]{2,1,0:T(8,128)(2,1)S(1)} %get-tuple-element.15), channel_id=1, replica_groups=mesh['ci'=8,'co'=16,'sp'=2] {'ci'}, dimensions={0} | all-to-all | bytes 655360 | tf_op jit(solution)/shard_map/all_to_all | solution.py:366
  43.1 0.0 copy-done.2
  43.1 0.0 copy-start.4
  43.1 1.9 %shard_map.78.own_ref = bf16[448,128]{1,0:T(8,128)(2,1)S(1)} custom-call(s32[1]{0:T(128)} %bitcast.side_ref, bf16[32,64,128]{2,1,0:T(8,128)(2,1)S(1)} %copy-done.2, bf16[8,160,128]{2,1,0:T(8,128)(2,1)S(1)} %all_to_all.16.gathered_ref), custom_call_target="tpu_custom_call" | custom-call | flops 452984832 | bytes 786432 | tf_op jit(solution)/shard_map/pallas_call | solution.py:367
  45.0 0.0 copy-done.4
  45.0 2.0 %shard_map.79 = bf16[32,64,128]{2,1,0:T(8,128)(2,1)} custom-call(s32[1]{0:T(128)} %bitcast.side_ref, bf16[8,160,128]{2,1,0:T(8,128)(2,1)S(1)} %all_to_all.16.gathered_ref, bf16[27,32,64]{2,1,0:T(8,128)(2,1)S(1)} %bitcast.7), custom_call_target="tpu_custom_call" | custom-call | flops 452984832 | bytes 786432 | tf_op jit(solution)/shard_map/pallas_call | solution.py:380
  47.0 11.3 %all-to-all-start.2 = ((bf16[16,2,64,128]{3,2,1,0:T(8,128)(2,1)}), bf16[16,2,64,128]{3,2,1,0:T(8,128)(2,1)S(1)}, u32[]{:S(2)}, u32[]{:S(2)}) async-start(bf16[16,2,64,128]{3,2,1,0:T(8,128)(2,1)} %bitcast.3), calls=%async_computation.2 | async-start | bytes 1048576 | tf_op jit(solution)/shard_map/all_to_all | solution.py:391
  58.3 0.3 collective-permute-start.1
  58.7 9.3 %collective-permute-done.1.other_ref = bf16[448,128]{1,0:T(8,128)(2,1)S(1)} collective-permute-done((bf16[448,128]{1,0:T(8,128)(2,1)S(1)}, bf16[448,128]{1,0:T(8,128)(2,1)S(1)}, u32[]{:S(2)}, u32[]{:S(2)}) %collective-permute-start.1) | collective-permute-done | bytes 114720 | tf_op jit(solution)/shard_map/ppermute | solution.py:378
  68.0 0.9 %shard_map.81 = (f32[27,32,64]{2,1,0:T(8,128)}, f32[1,32]{1,0:T(1,128)}) custom-call(bf16[448,128]{1,0:T(8,128)(2,1)S(1)} %shard_map.78.own_ref, bf16[448,128]{1,0:T(8,128)(2,1)S(1)} %collective-permute-done.1.other_ref), custom_call_target="tpu_custom_call" | custom-call | bytes 221184 | tf_op jit(solution)/shard_map/pallas_call | solution.py:401
  68.9 0.8 %all-to-all-done.2.shares_ref = bf16[16,2,64,128]{3,2,1,0:T(8,128)(2,1)S(1)} async-done(((bf16[16,2,64,128]{3,2,1,0:T(8,128)(2,1)}), bf16[16,2,64,128]{3,2,1,0:T(8,128)(2,1)S(1)}, u32[]{:S(2)}, u32[]{:S(2)}) %all-to-all-start.2) | async-done | bytes 524320 | tf_op jit(solution)/shard_map/all_to_all | solution.py:391
  69.6 0.7 %shard_map.80 = f32[2,64,128]{2,1,0:T(8,128)} custom-call(bf16[16,2,64,128]{3,2,1,0:T(8,128)(2,1)S(1)} %all-to-all-done.2.shares_ref), custom_call_target="tpu_custom_call" | custom-call | bytes 524288 | tf_op jit(solution)/shard_map/pallas_call | solution.py:394
Async XLA Ops:
  0.6 1.0 %copy-start.1 = (bf16[32,64,128]{2,1,0:T(8,128)(2,1)S(1)}, bf16[32,64,128]{2,1,0:T(8,128)(2,1)}, u32[]{:S(2)}) copy-start(bf16[32,64,128]{2,1,0:T(8,128)(2,1)} %features_ref.1) | copy-start | bytes 1572868
  1.7 0.9 %copy-start.3 = (bf16[27,64,32]{1,2,0:T(8,128)(2,1)S(1)}, bf16[27,64,32]{1,2,0:T(8,128)(2,1)}, u32[]{:S(2)}) copy-start(bf16[27,64,32]{1,2,0:T(8,128)(2,1)} %param.5) | copy-start | bytes 331780
  5.8 20.5 %copy-start = (bf16[4,32,128]{2,1,0:T(8,128)(2,1)S(1)}, bf16[4,32,128]{2,1,0:T(8,128)(2,1)}, u32[]{:S(2)}) copy-start(bf16[4,32,128]{2,1,0:T(8,128)(2,1)} %cotangent_ref.3) | copy-start | bytes 98308
  26.3 1.4 %copy-start.5 = (f32[32]{0:T(128)S(1)}, f32[32]{0:T(128)}, u32[]{:S(2)}) copy-start(f32[32]{0:T(128)} %param.6) | copy-start | bytes 388
  26.4 16.7 %copy-start.2 = (bf16[32,64,128]{2,1,0:T(8,128)(2,1)S(1)}, bf16[32,64,128]{2,1,0:T(8,128)(2,1)}, u32[]{:S(2)}) copy-start(bf16[32,64,128]{2,1,0:T(8,128)(2,1)} %features_ref.1) | copy-start | bytes 1572868
  26.4 3.0 %collective-permute-start = (f32[3,32,128]{2,1,0:T(8,128)S(1)}, f32[3,32,128]{2,1,0:T(8,128)S(1)}, u32[]{:S(2)}, u32[]{:S(2)}) collective-permute-start(f32[3,32,128]{2,1,0:T(8,128)S(1)} %get-tuple-element.13.mine_ref), channel_id=1, source_target_pairs={{0,1},{1,0},{2,3},{3,2},{4,5},{5,4},{6,7},{7,6},{8,9},{9,8},{10,11... | collective-permute-start | bytes 147464 | tf_op jit(solution)/shard_map/ppermute | solution.py:358
  43.1 1.9 %copy-start.4 = (bf16[27,64,32]{1,2,0:T(8,128)(2,1)S(1)}, bf16[27,64,32]{1,2,0:T(8,128)(2,1)}, u32[]{:S(2)}) copy-start(bf16[27,64,32]{1,2,0:T(8,128)(2,1)} %param.5) | copy-start | bytes 331780
  47.0 22.6 %all-to-all-start.2 = ((bf16[16,2,64,128]{3,2,1,0:T(8,128)(2,1)}), bf16[16,2,64,128]{3,2,1,0:T(8,128)(2,1)S(1)}, u32[]{:S(2)}, u32[]{:S(2)}) async-start(bf16[16,2,64,128]{3,2,1,0:T(8,128)(2,1)} %bitcast.3), calls=%async_computation.2 | async-start | bytes 1048576 | tf_op jit(solution)/shard_map/all_to_all | solution.py:391
  58.3 9.6 %collective-permute-start.1 = (bf16[448,128]{1,0:T(8,128)(2,1)S(1)}, bf16[448,128]{1,0:T(8,128)(2,1)S(1)}, u32[]{:S(2)}, u32[]{:S(2)}) collective-permute-start(bf16[448,128]{1,0:T(8,128)(2,1)S(1)} %shard_map.78.own_ref), channel_id=1, source_target_pairs={{0,1},{1,0},{2,3},{3,2},{4,5},{5,4},{6,7},{7,6},{8,9},{9,8},{10,11... | collective-permute-start | bytes 344072 | tf_op jit(solution)/shard_map/ppermute | solution.py:378

commit v2 on v1

--- a/solution.py
+++ b/solution.py
@@ -12,9 +12,10 @@
 VMEM = pl.BlockSpec(memory_space=pltpu.VMEM)
 SMEM = pl.BlockSpec(memory_space=pltpu.SMEM)
 HBM = pl.BlockSpec(memory_space=pltpu.HBM)
-
-
-def call(body, outs, specs, flops, moved, scratch=()):
+stay = pltpu.with_memory_space_constraint
+
+
+def call(body, outs, specs, flops, moved, scratch=(), vmem=40):
     return pl.pallas_call(
         body,
         out_shape=outs,
@@ -22,7 +23,7 @@
         out_specs=jax.tree.map(lambda _: VMEM, outs),
         scratch_shapes=list(scratch),
         cost_estimate=pl.CostEstimate(flops=flops, bytes_accessed=moved, transcendentals=0),
-        compiler_params=pltpu.CompilerParams(vmem_limit_bytes=40 * 2**20),
+        compiler_params=pltpu.CompilerParams(vmem_limit_bytes=vmem * 2**20),
     )
 
 
@@ -69,15 +70,14 @@
     return parts
 
 
-def correlate_rows(taps, spread_ref, y, width, store):
+def correlate_rows(taps, spread_ref, y, width):
     depth = 3 * spread_ref.shape[1]
     columns = jnp.concatenate(
-        [spread_ref[y + k : y + k + 3].reshape(depth, LANES) for k in range(2)], axis=1
+        [spread_ref[pl.ds(y + k, 3)].reshape(depth, LANES) for k in range(2)], axis=1
     )
     product = jnp.dot(taps, columns, preferred_element_type=F32)
     parts = along_z([product[c * width : (c + 1) * width] for c in range(3)])
-    for k in range(2):
-        store(y + k, parts[k].astype(BF16))
+    return [part.astype(BF16) for part in parts]
 
 
 def forward(
@@ -113,10 +113,6 @@
         )
     taps = taps_ref[...]
 
-    def store(y, value):
-        start = y % 4 * width_out
-        out_ref[y // 4, start : start + width_out] = value
-
     done = 0
     for group in range(groups):
         if group * 4 % step == 0:
@@ -128,7 +124,10 @@
                 spread_ref[4 * group + k + 1, b * width_in : (b + 1) * width_in] = seen[b]
         edge_ref[group + 1] = pack_plane(side, planes)
         while done + 2 < 4 * group + 4 or (group == groups - 1 and done < rows_y):
-            correlate_rows(taps, spread_ref, done, width_out, store)
+            parts = correlate_rows(taps, spread_ref, done, width_out)
+            for k in range(2):
+                start = (done + k) % 4 * width_out
+                out_ref[done // 4, start : start + width_out] = parts[k]
             done += 2
     none = jnp.zeros(edge_ref.shape[1:], BF16)
     edge_ref[0] = none
@@ -166,31 +165,36 @@
     message_ref[2] = pack_plane(side, [cotangent_ref[k].astype(F32) for k in range(rows)])
 
 
-def gelu(pre, cotangent):
-    scale, cubic = 0.7978845608, 0.044715
-    square = pre * pre
-    bend = jnp.tanh(scale * (pre + cubic * (square * pre)))
-    half = 0.5 * (1.0 + bend)
-    slope = half + 0.5 * pre * (1.0 - bend * bend) * (scale * (1.0 + 3.0 * cubic * square))
-    return (pre * half).astype(BF16), (cotangent * slope).astype(BF16)
-
-
-def pointwise(side_ref, own_ref, mine_ref, theirs_ref, bias_ref, cotangent_ref, act_ref, out_ref):
-    rows, width, _ = own_ref.shape
-    side = side_ref[0]
-    bias = jnp.broadcast_to(bias_ref[...], (width, LANES))
-    at = lane((width, LANES))
-    edge = at // SZ == 3 * (1 - side)
+def bend(pre):
+    return jnp.tanh(0.7978845608 * (pre + 0.044715 * (pre * pre * pre)))
+
+
+def gelu_slope(pre, cotangent):
+    bent = bend(pre)
+    inner = 0.7978845608 * (1.0 + 3.0 * 0.044715 * (pre * pre))
+    slope = 0.5 * (1.0 + bent) + 0.5 * pre * (1.0 - bent * bent) * inner
+    return (cotangent * slope).astype(BF16)
+
+
+def preactivation(side, own_ref, theirs_ref, bias):
+    width = own_ref.shape[1]
+    edge = lane((width, LANES)) // SZ == 3 * (1 - side)
     added = theirs_ref[0]
-    grads = []
-    for k in range(rows):
+    rows = []
+    for k in range(own_ref.shape[0]):
         moved = pltpu.roll(added, lax.rem(3 * SZ * (1 - side) - SZ * k + LANES, LANES), 1)
-        pre = own_ref[k] + jnp.where(edge, moved, 0.0) + bias
-        act, grad = gelu(pre, cotangent_ref[k].astype(F32))
-        act_ref[k] = act
-        grads.append(grad)
-    _, grad = gelu(theirs_ref[1] + mine_ref[0] + bias, theirs_ref[2])
-    block = jnp.concatenate(grads + [grad], axis=0)
+        rows.append(own_ref[k] + jnp.where(edge, moved, 0.0) + bias)
+    return rows
+
+
+def pointwise(side_ref, own_ref, mine_ref, theirs_ref, bias_ref, cotangent_ref, out_ref):
+    bias = jnp.broadcast_to(bias_ref[...], own_ref.shape[1:])
+    grads = [
+        gelu_slope(pre, cotangent_ref[k].astype(F32))
+        for k, pre in enumerate(preactivation(side_ref[0], own_ref, theirs_ref, bias))
+    ]
+    grads.append(gelu_slope(theirs_ref[1] + mine_ref[0] + bias, theirs_ref[2]))
+    block = jnp.concatenate(grads, axis=0)
     for k in range(out_ref.shape[0]):
         out_ref[k] = block
 
@@ -204,9 +208,13 @@
             put(4 * group + k, neighbours(own, low, high, k))
 
 
-def backward(side_ref, gathered_ref, weight_ref, out_ref, spread_ref, taps_ref):
-    rows_y, width_in, _ = out_ref.shape
+def backward(
+    side_ref, core_ref, gathered_ref, weight_ref, mine_ref, other_ref, spread_ref, taps_ref
+):
+    slots, rows, width_in, _ = mine_ref.shape
+    rows_y = 2 * slots * rows
     width_out = weight_ref.shape[1]
+    core = core_ref[0]
     blank = jnp.zeros(spread_ref.shape[1:], BF16)
     spread_ref[0] = blank
     spread_ref[rows_y + 1] = blank
@@ -219,13 +227,17 @@
     for c in range(3):
         block = jnp.concatenate([weight_ref[26 - 3 * ab - c] for ab in range(9)], axis=0)
         taps_ref[c * width_in : (c + 1) * width_in] = block.T
-
-    def store(y, value):
-        out_ref[y] = value
-
     taps = taps_ref[...]
-    for y in range(0, rows_y, 2):
-        correlate_rows(taps, spread_ref, y, width_in, store)
+    for out_ref, owner in ((other_ref, 1 - core), (mine_ref, core)):
+        for slot in range(slots):
+            parts = correlate_rows(taps, spread_ref, 2 * rows * slot + rows * owner, width_in)
+            for k in range(rows):
+                out_ref[slot, k] = parts[k]
+
+
+def add_pair(core_ref, mine_ref, others_ref, out_ref):
+    other = others_ref[1 - core_ref[0]]
+    out_ref[...] = (mine_ref[...].astype(F32) + other.astype(F32)).astype(BF16)
 
 
 def filter_gradient(side_ref, features_ref, gathered_ref, out_ref, grad_ref, rows_ref):
@@ -286,7 +298,17 @@
     )
 
 
-def finish_filter(own_ref, other_ref, weight_ref, bias_ref):
+def finish(
+    side_ref, shares_ref, own_ref, other_ref, sums_ref, theirs_ref, bias_vector_ref,
+    input_ref, weight_ref, bias_ref, act_ref,
+):
+    total = shares_ref[0].astype(F32)
+    for k in range(1, shares_ref.shape[0]):
+        total = total + shares_ref[k].astype(F32)
+    input_ref[...] = total
+    bias = jnp.broadcast_to(bias_vector_ref[...], sums_ref.shape[1:])
+    for k, pre in enumerate(preactivation(side_ref[0], sums_ref, theirs_ref, bias)):
+        act_ref[k] = (0.5 * pre * (1.0 + bend(pre))).astype(BF16)
     _, width_out, width_in = weight_ref.shape
     count = 9 * width_out
     half = count // 2
@@ -312,19 +334,14 @@
     )[:, :width_out]
 
 
-def add_shares(shares_ref, out_ref):
-    total = shares_ref[0].astype(F32)
-    for k in range(1, shares_ref.shape[0]):
-        total = total + shares_ref[k].astype(F32)
-    out_ref[...] = total
-
-
 def local(features, weight, bias_vector, cotangent):
     rows_y, width_in, _ = features.shape
     width_out = weight.shape[2]
     n_ci, n_co = lax.axis_size("ci"), lax.axis_size("co")
     shape = jax.ShapeDtypeStruct
     side = lax.axis_index("sp").astype(jnp.int32).reshape(1)
+    core = lax.rem(lax.axis_index("co"), 2).astype(jnp.int32).reshape(1)
+    side, core = lax.optimization_barrier((side, core))
     swap = [(0, 1), (1, 0)]
     taps = weight.transpose(0, 2, 1)
     work = 2 * 27 * rows_y * LANES * width_in * width_out
@@ -333,7 +350,7 @@
     block = 5 * width_out
     partial = call(
         forward,
-        shape((n_ci, block, LANES), BF16),
+        pltpu.VMEM((n_ci, block, LANES), BF16),
         [SMEM, HBM, HBM],
         work,
         size * (width_in + width_out),
@@ -344,9 +361,9 @@
             pltpu.VMEM((3 * width_out, 9 * width_in), BF16),
             pltpu.VMEM((3 * width_out, 3 * width_in), BF16),
             pltpu.VMEM((rows_y // 4 + 2, width_in, LANES), BF16),
-            pltpu.SemaphoreType.DMA((5,)),
+            pltpu.SemaphoreType.DMA((2,)),
         ],
-    )(side, features, taps)
+    )(side, stay(features, pltpu.HBM), stay(taps, pltpu.HBM))
     shares = lax.all_to_all(partial, "ci", 0, 0, tiled=True)
     own, mine = call(
         reduce_rows,
@@ -356,13 +373,14 @@
         2 * size * width_out,
     )(side, shares, cotangent)
     theirs = lax.ppermute(mine, "sp", swap)
-    activated, copies = call(
+    bias_column = bias_vector.reshape(width_out, 1)
+    copies = call(
         pointwise,
-        (shape(cotangent.shape, BF16), shape((n_ci, block, LANES), BF16)),
+        pltpu.VMEM((n_ci, block, LANES), BF16),
         [SMEM, VMEM, VMEM, VMEM, VMEM, VMEM],
         0,
         2 * size * width_out,
-    )(side, own, mine, theirs, bias_vector.reshape(width_out, 1), cotangent)
+    )(side, own, mine, theirs, bias_column, cotangent)
     gathered = lax.all_to_all(copies, "ci", 0, 0, tiled=True)
     packed = call(
         filter_gradient,
@@ -377,34 +395,38 @@
     )(side, features, gathered)
     other = lax.ppermute(packed, "sp", swap)
     gathered, packed = lax.optimization_barrier((gathered, packed))
-    shares = call(
+    quarter = (n_co // 2, rows_y // n_co, width_in, LANES)
+    mine, other_half = call(
         backward,
-        shape((rows_y, width_in, LANES), BF16),
-        [SMEM, VMEM, VMEM],
+        (pltpu.VMEM(quarter, BF16), pltpu.VMEM(quarter, BF16)),
+        [SMEM, SMEM, VMEM, VMEM],
         work,
         size * (width_in + width_out),
         [
             pltpu.VMEM((rows_y + 2, 3 * width_out, LANES), BF16),
             pltpu.VMEM((3 * width_in, 9 * width_out), BF16),
         ],
-    )(side, gathered, taps)
-    shares = lax.all_to_all(
-        shares.reshape(n_co, rows_y // n_co, width_in, LANES), "co", 0, 0, tiled=True
-    )
-    input_grad = call(
-        add_shares,
-        shape((rows_y // n_co, width_in, LANES), F32),
-        [VMEM],
-        0,
-        size * width_in,
-    )(shares)
-    weight_grad, bias_grad = call(
-        finish_filter,
-        (shape((27, width_out, width_in), F32), shape((1, width_out), F32)),
-        [VMEM, VMEM],
+    )(side, core, gathered, taps)
+    pairs = [[k, k + 1] for k in range(0, n_co, 2)]
+    halves = lax.all_gather(other_half, "co", axis=0, axis_index_groups=pairs)
+    summed = call(
+        add_pair, pltpu.VMEM(quarter, BF16), [SMEM, VMEM, VMEM], 0, size * width_in
+    )(core, mine, halves)
+    summed, other = lax.optimization_barrier((summed, other))
+    same_core = [list(range(k, n_co, 2)) for k in range(2)]
+    shares = lax.all_to_all(summed, "co", 0, 0, tiled=True, axis_index_groups=same_core)
+    input_grad, weight_grad, bias_grad, activated = call(
+        finish,
+        (
+            shape(quarter[1:], F32),
+            shape((27, width_out, width_in), F32),
+            shape((1, width_out), F32),
+            shape(cotangent.shape, BF16),
+        ),
+        [SMEM] + [VMEM] * 6,
         0,
         27 * 4 * width_in * width_out,
-    )(packed, other)
+    )(side, shares, packed, other, own, theirs, bias_column)
     return (activated, input_grad, weight_grad.transpose(0, 2, 1), bias_grad.reshape(width_out))
 
 

time: 70.7 us -> 66.3 us (0.938)
  blocking collectives: 33.4 us -> 53.9 us
  starting transfers between devices: 12.9 us -> 2.57 us
  waiting for transfers between devices: 11.7 us -> 1.66 us
  Pallas kernels: 9.56 us -> 7.05 us
  local copies, waits for them, and re-layouts: 2.08 us -> 0.11 us
    all_to_all x0 -> x1, blocking collectives: none -> 14.1 us  [local(): lax.all_to_all(summed, 'co', 0, 0, tiled=True, axis_index_groups=same_core)]
    all_to_all x1 -> x0, starting transfers between devices: 11.3 us -> none  [local(): lax.all_to_all(shares.reshape(n_co, rows_y // n_co, width_in, LANES), 'co...]
    ppermute x1, waiting for transfers between devices: 9.33 us -> 0.01 us  [local(): other = lax.ppermute(packed, 'sp', swap)]
    all_gather x0 -> x1, blocking collectives: none -> 6.46 us  [local(): halves = lax.all_gather(other_half, 'co', axis=0, axis_index_groups=pairs)]
    pallas_call x5, Pallas kernels: 7.57 us -> 5.05 us  [the longest x1 2.54 us: local(): call(forward, pltpu.VMEM((n_ci, block, LANES), BF16), [SMEM, HBM, HBM], w...]
    unnamed x12 -> x8, local copies, waits for them, and re-layouts: 1.99 us -> 0.02 us
    ppermute x1, starting transfers between devices: 0.31 us -> 1.29 us  [local(): other = lax.ppermute(packed, 'sp', swap)]
    all_to_all x1 -> x0, waiting for transfers between devices: 0.77 us -> none  [local(): lax.all_to_all(shares.reshape(n_co, rows_y // n_co, width_in, LANES), 'co...]
  transfers between devices with their start and end apart: 3 -> 2, of which waited for: 3 -> 1; matrix products, arithmetic and copies ran while one was open for 0% -> 0% of each run, Pallas kernels for 1% -> 2%
where the time goes in v2:
time: 66.3 us; the launch traced here: 66 us
  blocking collectives  53.9 us (81%)
  Pallas kernels  7.05 us (11%)
  starting transfers between devices  2.57 us (4%)
  waiting for transfers between devices  1.66 us (3%)
  between operations  0.7 us (1%)
    all_to_all x1, blocking collectives, local(): shares = lax.all_to_all(partial, 'ci', 0, 0, tiled=True)  20.5 us
    all_to_all x1, blocking collectives, local(): lax.all_to_all(summed, 'co', 0, 0, tiled=True, axis_index_groups=same_core)  14.1 us
    all_to_all x1, blocking collectives, local(): gathered = lax.all_to_all(copies, 'ci', 0, 0, tiled=True)  12.9 us
    all_gather x1, blocking collectives, local(): halves = lax.all_gather(other_half, 'co', axis=0, axis_index_groups=pairs)  6.46 us
    pallas_call x1, Pallas kernels, local(): call(forward, pltpu.VMEM((n_ci, block, LANES), BF16), [SMEM, HBM, HBM], w...  2.54 us
    pallas_call x1, Pallas kernels, local(): call(filter_gradient, shape((9 * width_out + 9 * width_out // 2 + 16, LAN...  1.89 us
    ppermute x1, waiting for transfers between devices, local(): theirs = lax.ppermute(mine, 'sp', swap)  1.66 us
    pallas_call x1, Pallas kernels, local(): call(backward, (pltpu.VMEM(quarter, BF16), pltpu.VMEM(quarter, BF16)), [S...  1.38 us
  transfers between devices with their start and end apart: 2, of which 1 were waited for; matrix products, arithmetic and copies ran while one was open for 0% of the time, Pallas kernels for 2%

profile of v2, /device:TPU:1, one launch (start us, length us, event | category | flops | bytes accessed | tf_op | source)
XLA Modules:
  0.0 66.0 jit_solution(5118080411845096399)
XLA Ops:
  0.6 2.5 %shard_map.75 = bf16[8,160,128]{2,1,0:T(8,128)(2,1)S(1)} custom-call(s32[1]{0:T(128)} %bitcast.side_ref, bf16[32,64,128]{2,1,0:T(8,128)(2,1)} %features_ref.1, bf16[27,32,64]{2,1,0:T(8,128)(2,1)} %bitcast.8), custom_call_target="tpu_custom_call" | custom-call | flops 452984832 | bytes 786432 | tf_op jit(solution)/shard_map/pallas_call | solution.py:351
  3.2 0.0 copy-start
  3.2 20.5 %all_to_all.15.shares_ref = bf16[8,160,128]{2,1,0:T(8,128)(2,1)S(1)} all-to-all(bf16[8,160,128]{2,1,0:T(8,128)(2,1)S(1)} %shard_map.75), channel_id=1, replica_groups=mesh['ci'=8,'co'=16,'sp'=2] {'ci'}, dimensions={0} | all-to-all | bytes 655360 | tf_op jit(solution)/shard_map/all_to_all | solution.py:367
  23.7 0.0 copy-done
  23.7 0.1 shard_map.76
  23.8 0.0 copy-start.3
  23.8 1.3 %collective-permute-start = (f32[3,32,128]{2,1,0:T(8,128)S(1)}, f32[3,32,128]{2,1,0:T(8,128)S(1)}, u32[]{:S(2)}, u32[]{:S(2)}) collective-permute-start(f32[3,32,128]{2,1,0:T(8,128)S(1)} %get-tuple-element.21.mine_ref), channel_id=1, source_target_pairs={{0,1},{1,0},{2,3},{3,2},{4,5},{5,4},{6,7},{7,6},{8,9},{9,8},{10,11... | collective-permute-start | bytes 147464 | tf_op jit(solution)/shard_map/ppermute | solution.py:375
  25.1 0.0 copy-done.3
  25.1 0.1 copy.10.bias_ref.bias_vector_ref
  25.2 1.7 %collective-permute-done.theirs_ref = f32[3,32,128]{2,1,0:T(8,128)S(1)} collective-permute-done((f32[3,32,128]{2,1,0:T(8,128)S(1)}, f32[3,32,128]{2,1,0:T(8,128)S(1)}, u32[]{:S(2)}, u32[]{:S(2)}) %collective-permute-start) | collective-permute-done | bytes 49184 | tf_op jit(solution)/shard_map/ppermute | solution.py:375
  26.8 0.0 copy-start.1
  26.9 0.1 shard_map.77
  27.0 12.9 %all_to_all.16.gathered_ref = bf16[8,160,128]{2,1,0:T(8,128)(2,1)S(1)} all-to-all(bf16[8,160,128]{2,1,0:T(8,128)(2,1)S(1)} %shard_map.77), channel_id=1, replica_groups=mesh['ci'=8,'co'=16,'sp'=2] {'ci'}, dimensions={0} | all-to-all | bytes 655360 | tf_op jit(solution)/shard_map/all_to_all | solution.py:384
  39.9 0.0 copy-done.1
  39.9 0.0 copy-start.2
  39.9 1.9 %shard_map.78.own_ref = bf16[448,128]{1,0:T(8,128)(2,1)S(1)} custom-call(s32[1]{0:T(128)} %bitcast.side_ref, bf16[32,64,128]{2,1,0:T(8,128)(2,1)S(1)} %copy-done.1, bf16[8,160,128]{2,1,0:T(8,128)(2,1)S(1)} %all_to_all.16.gathered_ref), custom_call_target="tpu_custom_call" | custom-call | flops 452984832 | bytes 786432 | tf_op jit(solution)/shard_map/pallas_call | solution.py:385
  41.8 1.3 %collective-permute-start.1 = (bf16[448,128]{1,0:T(8,128)(2,1)S(1)}, bf16[448,128]{1,0:T(8,128)(2,1)S(1)}, u32[]{:S(2)}, u32[]{:S(2)}) collective-permute-start(bf16[448,128]{1,0:T(8,128)(2,1)S(1)} %shard_map.78.own_ref), channel_id=1, source_target_pairs={{0,1},{1,0},{2,3},{3,2},{4,5},{5,4},{6,7},{7,6},{8,9},{9,8},{10,11... | collective-permute-start | bytes 344072 | tf_op jit(solution)/shard_map/ppermute | solution.py:396
  43.1 0.0 copy-done.2
  43.1 1.4 %shard_map.79 = (bf16[8,2,64,128]{3,2,1,0:T(8,128)(2,1)S(1)}, bf16[8,2,64,128]{3,2,1,0:T(8,128)(2,1)S(1)}) custom-call(s32[1]{0:T(128)} %bitcast.side_ref, s32[1]{0:T(128)} %bitcast.1.core_ref, bf16[8,160,128]{2,1,0:T(8,128)(2,1)S(1)} %all_to_all.16.gathered_ref, bf16[27,32,64]{2,1,0:T(8,128)(2,1)S(1)} %bitcast.9), custom_call_target="tpu_custom_call" | custom-call | flops 452984832 | bytes 786432 | tf_op jit(solution)/shard_map/pallas_call | solution.py:399
  44.5 6.5 %all-gather = bf16[16,2,64,128]{3,2,1,0:T(8,128)(2,1)S(1)} all-gather(bf16[8,2,64,128]{3,2,1,0:T(8,128)(2,1)S(1)} %get-tuple-element.24), channel_id=2, replica_groups={{0,2},{4,6},{8,10},{12,14},{16,18},{20,22},{24,26},{28,30},{1,3},{5,7},..., dimensions={0}, use_global_device_ids=true | all-gather | bytes 786432 | tf_op jit(solution)/shard_map/all_gather | solution.py:411
  50.9 0.1 shard_map.80
  51.0 0.0 collective-permute-done.1.other_ref
  51.0 14.1 %all_to_all.17.shares_ref = bf16[8,2,64,128]{3,2,1,0:T(8,128)(2,1)S(1)} all-to-all(bf16[8,2,64,128]{3,2,1,0:T(8,128)(2,1)S(1)} %shard_map.80), channel_id=1, replica_groups={{0,4,8,12,16,20,24,28},{2,6,10,14,18,22,26,30},{1,5,9,13,17,21,25,29},{..., dimensions={0} | all-to-all | bytes 524288 | tf_op jit(solution)/shard_map/all_to_all | solution.py:417
  65.1 0.9 %shard_map.81 = (f32[2,64,128]{2,1,0:T(8,128)}, f32[27,32,64]{2,1,0:T(8,128)}, f32[1,32]{1,0:T(1,128)}, bf16[4,32,128]{2,1,0:T(8,128)(2,1)}) custom-call(s32[1]{0:T(128)} %bitcast.side_ref, bf16[8,2,64,128]{3,2,1,0:T(8,128)(2,1)S(1)} %all_to_all.17.shares_ref, bf16[448,128]{1,0:T(8,128)(2,1)S(1)} %shard_map.78.own_ref, ...), custom_call_target="tpu_custom_call" | custom-call | bytes 221184 | tf_op jit(solution)/shard_map/pallas_call | solution.py:418
Async XLA Ops:
  3.2 20.5 %copy-start = (bf16[4,32,128]{2,1,0:T(8,128)(2,1)S(1)}, bf16[4,32,128]{2,1,0:T(8,128)(2,1)}, u32[]{:S(2)}) copy-start(bf16[4,32,128]{2,1,0:T(8,128)(2,1)} %cotangent_ref.3) | copy-start | bytes 98308
  23.8 1.3 %copy-start.3 = (f32[32]{0:T(128)S(1)}, f32[32]{0:T(128)}, u32[]{:S(2)}) copy-start(f32[32]{0:T(128)} %param.6) | copy-start | bytes 388
  23.8 3.0 %collective-permute-start = (f32[3,32,128]{2,1,0:T(8,128)S(1)}, f32[3,32,128]{2,1,0:T(8,128)S(1)}, u32[]{:S(2)}, u32[]{:S(2)}) collective-permute-start(f32[3,32,128]{2,1,0:T(8,128)S(1)} %get-tuple-element.21.mine_ref), channel_id=1, source_target_pairs={{0,1},{1,0},{2,3},{3,2},{4,5},{5,4},{6,7},{7,6},{8,9},{9,8},{10,11... | collective-permute-start | bytes 147464 | tf_op jit(solution)/shard_map/ppermute | solution.py:375
  26.8 13.1 %copy-start.1 = (bf16[32,64,128]{2,1,0:T(8,128)(2,1)S(1)}, bf16[32,64,128]{2,1,0:T(8,128)(2,1)}, u32[]{:S(2)}) copy-start(bf16[32,64,128]{2,1,0:T(8,128)(2,1)} %features_ref.1) | copy-start | bytes 1572868
  39.9 3.2 %copy-start.2 = (bf16[27,64,32]{1,2,0:T(8,128)(2,1)S(1)}, bf16[27,64,32]{1,2,0:T(8,128)(2,1)}, u32[]{:S(2)}) copy-start(bf16[27,64,32]{1,2,0:T(8,128)(2,1)} %param.5) | copy-start | bytes 331780
  41.8 9.2 %collective-permute-start.1 = (bf16[448,128]{1,0:T(8,128)(2,1)S(1)}, bf16[448,128]{1,0:T(8,128)(2,1)S(1)}, u32[]{:S(2)}, u32[]{:S(2)}) collective-permute-start(bf16[448,128]{1,0:T(8,128)(2,1)S(1)} %shard_map.78.own_ref), channel_id=1, source_target_pairs={{0,1},{1,0},{2,3},{3,2},{4,5},{5,4},{6,7},{7,6},{8,9},{9,8},{10,11... | collective-permute-start | bytes 344072 | tf_op jit(solution)/shard_map/ppermute | solution.py:396

commit v3 on v2

--- a/solution.py
+++ b/solution.py
@@ -40,19 +40,33 @@
     return packed
 
 
-def neighbours(own, low=None, high=None, k=0):
+def neighbours(own, left=None, right=None):
     at = lane(own.shape)
     zero = jnp.zeros_like(own)
-    left = zero if low is None else pltpu.roll(low, (-SZ * k) % LANES, 1)
-    right = zero if high is None else pltpu.roll(high, (LANES - SZ - SZ * k) % LANES, 1)
-    before = jnp.where(at < SZ, left, pltpu.roll(own, SZ, 1))
-    after = jnp.where(at >= LANES - SZ, right, pltpu.roll(own, LANES - SZ, 1))
+    before = jnp.where(at < SZ, zero if left is None else left, pltpu.roll(own, SZ, 1))
+    after = jnp.where(
+        at >= LANES - SZ, zero if right is None else right, pltpu.roll(own, LANES - SZ, 1)
+    )
     return before, own, after
 
 
-def split_halo(side, packed):
-    zero = jnp.zeros_like(packed)
-    return jnp.where(side == 1, packed, zero), jnp.where(side == 0, packed, zero)
+def unpack_row(packed, row, target):
+    half = LANES // 2
+    return jnp.concatenate(
+        [pltpu.roll(packed, (target - h * half - SZ * row) % LANES, 1) for h in range(2)], axis=0
+    )
+
+
+def pack_rows(rows, source):
+    half = rows[0].shape[0] // 2
+    at = lane((half, LANES))
+    packed = None
+    for k in range(4):
+        h, row = divmod(k, 2)
+        piece = rows[row][h * half : (h + 1) * half]
+        moved = pltpu.roll(piece, (SZ * k - source) % LANES, 1)
+        packed = moved if k == 0 else jnp.where(at >= SZ * k, moved, packed)
+    return packed
 
 
 def along_z(terms):
@@ -81,25 +95,18 @@
 
 
 def forward(
-    side_ref, features_hbm, weight_hbm, out_ref,
-    features_ref, weight_ref, spread_ref, taps_ref, edge_taps_ref, edge_ref, sems,
+    side_ref, features_hbm, weight_hbm, bias_hbm, out_ref, column_ref,
+    features_ref, weight_ref, bias_ref, spread_ref, taps_ref, edge_taps_ref, edge_ref, sems,
 ):
     rows_y, width_in, _ = features_ref.shape
     width_out = weight_ref.shape[1]
     groups = rows_y // 4
-    pieces = sems.shape[0] - 1
-    step = rows_y // pieces
-    fetch = [
-        pltpu.make_async_copy(
-            features_hbm.at[pl.ds(k * step, step)], features_ref.at[pl.ds(k * step, step)], sems.at[k]
-        )
-        for k in range(pieces)
-    ]
-    fetch_weight = pltpu.make_async_copy(weight_hbm, weight_ref, sems.at[pieces])
-    fetch[0].start()
+    fetch_weight = pltpu.make_async_copy(weight_hbm, weight_ref, sems.at[0])
+    fetch = pltpu.make_async_copy(features_hbm, features_ref, sems.at[1])
+    fetch_bias = pltpu.make_async_copy(bias_hbm, bias_ref, sems.at[2])
     fetch_weight.start()
-    for copy in fetch[1:]:
-        copy.start()
+    fetch.start()
+    fetch_bias.start()
     side = side_ref[0]
     blank = jnp.zeros(spread_ref.shape[1:], BF16)
     spread_ref[0] = blank
@@ -112,11 +119,14 @@
             [weight_ref[9 * a + c + 6 * side] for a in range(3)], axis=1
         )
     taps = taps_ref[...]
-
+    fetch_bias.wait()
+    shape = (width_out, width_out)
+    diagonal = lax.broadcasted_iota(jnp.int32, shape, 0) == lane(shape)
+    column = jnp.sum(jnp.where(diagonal, bias_ref[...], 0.0), axis=1, keepdims=True)
+    column_ref[...] = jnp.broadcast_to(column, column_ref.shape)
+    fetch.wait()
     done = 0
     for group in range(groups):
-        if group * 4 % step == 0:
-            fetch[group * 4 // step].wait()
         planes = [features_ref[4 * group + k] for k in range(4)]
         for k in range(4):
             seen = neighbours(planes[k])
@@ -126,8 +136,7 @@
         while done + 2 < 4 * group + 4 or (group == groups - 1 and done < rows_y):
             parts = correlate_rows(taps, spread_ref, done, width_out)
             for k in range(2):
-                start = (done + k) % 4 * width_out
-                out_ref[done // 4, start : start + width_out] = parts[k]
+                out_ref[done // 2, k * width_out : (k + 1) * width_out] = parts[k]
             done += 2
     none = jnp.zeros(edge_ref.shape[1:], BF16)
     edge_ref[0] = none
@@ -147,65 +156,75 @@
         edge_taps_ref[...], jnp.concatenate(columns, axis=1), preferred_element_type=F32
     )
     parts = along_z([product[c * width_out : (c + 1) * width_out] for c in range(3)])
+    half = width_out // 2
+    low = lane((half, LANES)) < LANES // 2
     for group in range(groups):
-        out_ref[group, 4 * width_out :] = parts[group].astype(BF16)
-
-
-def reduce_rows(side_ref, shares_ref, cotangent_ref, own_ref, message_ref):
-    total = shares_ref[0].astype(F32)
-    for k in range(1, shares_ref.shape[0]):
-        total = total + shares_ref[k].astype(F32)
-    rows, width, _ = cotangent_ref.shape
-    planes = [total[k * width : (k + 1) * width] for k in range(rows)]
-    for k in range(rows):
-        own_ref[k] = planes[k]
-    side = side_ref[0]
-    message_ref[0] = total[rows * width :]
-    message_ref[1] = pack_plane(side, planes)
-    message_ref[2] = pack_plane(side, [cotangent_ref[k].astype(F32) for k in range(rows)])
+        here = parts[group]
+        turned = pltpu.roll(here, LANES // 2, 1)
+        first = jnp.where(low, here[:half], turned[half:])
+        second = jnp.where(low, turned[:half], here[half:])
+        out_ref[2 * group, 2 * width_out :] = first.astype(BF16)
+        out_ref[2 * group + 1, 2 * width_out :] = second.astype(BF16)
 
 
 def bend(pre):
     return jnp.tanh(0.7978845608 * (pre + 0.044715 * (pre * pre * pre)))
 
 
-def gelu_slope(pre, cotangent):
+def gelu(pre, cotangent):
     bent = bend(pre)
+    half = 0.5 * (1.0 + bent)
     inner = 0.7978845608 * (1.0 + 3.0 * 0.044715 * (pre * pre))
-    slope = 0.5 * (1.0 + bent) + 0.5 * pre * (1.0 - bent * bent) * inner
-    return (cotangent * slope).astype(BF16)
-
-
-def preactivation(side, own_ref, theirs_ref, bias):
+    slope = half + 0.5 * pre * (1.0 - bent * bent) * inner
+    return (pre * half).astype(BF16), (cotangent.astype(F32) * slope).astype(BF16)
+
+
+def pointwise(side_ref, shares_ref, bias_ref, own_ref, other_ref, act_ref, out_ref):
     width = own_ref.shape[1]
-    edge = lane((width, LANES)) // SZ == 3 * (1 - side)
-    added = theirs_ref[0]
-    rows = []
-    for k in range(own_ref.shape[0]):
-        moved = pltpu.roll(added, lax.rem(3 * SZ * (1 - side) - SZ * k + LANES, LANES), 1)
-        rows.append(own_ref[k] + jnp.where(edge, moved, 0.0) + bias)
-    return rows
-
-
-def pointwise(side_ref, own_ref, mine_ref, theirs_ref, bias_ref, cotangent_ref, out_ref):
-    bias = jnp.broadcast_to(bias_ref[...], own_ref.shape[1:])
-    grads = [
-        gelu_slope(pre, cotangent_ref[k].astype(F32))
-        for k, pre in enumerate(preactivation(side_ref[0], own_ref, theirs_ref, bias))
+    lower, upper = side_ref[0] == 0, side_ref[0] == 1
+    bias = bias_ref[...]
+    sums = []
+    for h in range(2):
+        total = shares_ref[h].astype(F32)
+        for k in range(2 + h, shares_ref.shape[0], 2):
+            total = total + shares_ref[k].astype(F32)
+        sums.append(total)
+    at = lane((width, LANES))
+    edges = (at >= LANES - SZ, at < SZ)
+    grads = ([], [])
+    for row in range(2):
+        mine = own_ref[2 * side_ref[0] + row]
+        theirs = other_ref[2 * side_ref[0] + row]
+        cotangents = (jnp.where(lower, mine, theirs), jnp.where(upper, mine, theirs))
+        acts = []
+        for h in range(2):
+            added = unpack_row(sums[1 - h][2 * width :], row, (LANES - SZ, 0)[h])
+            pre = sums[h][row * width : (row + 1) * width]
+            pre = pre + jnp.where(edges[h], added, 0.0) + bias
+            act, grad = gelu(pre, cotangents[h])
+            acts.append(act)
+            grads[h].append(grad)
+        act_ref[0, row] = jnp.where(lower, acts[0], acts[1])
+        act_ref[1, row] = jnp.where(lower, acts[1], acts[0])
+    blocks = [
+        jnp.concatenate([*grads[h], pack_rows(grads[1 - h], (0, LANES - SZ)[h])], axis=0)
+        for h in range(2)
     ]
-    grads.append(gelu_slope(theirs_ref[1] + mine_ref[0] + bias, theirs_ref[2]))
-    block = jnp.concatenate(grads, axis=0)
     for k in range(out_ref.shape[0]):
-        out_ref[k] = block
+        out_ref[k] = blocks[k % 2]
 
 
 def spread_gradient(side, gathered_ref, width, put):
-    rows = 4 * width
-    for group in range(gathered_ref.shape[0]):
-        low, high = split_halo(side, gathered_ref[group, rows:])
-        for k in range(4):
-            own = gathered_ref[group, k * width : (k + 1) * width]
-            put(4 * group + k, neighbours(own, low, high, k))
+    for slot in range(gathered_ref.shape[0]):
+        packed = gathered_ref[slot, 2 * width :]
+        zero = jnp.zeros_like(packed)
+        low = jnp.where(side == 1, packed, zero)
+        high = jnp.where(side == 0, packed, zero)
+        for row in range(2):
+            own = gathered_ref[slot, row * width : (row + 1) * width]
+            left = unpack_row(low, row, 0)
+            right = unpack_row(high, row, LANES - SZ)
+            put(2 * slot + row, neighbours(own, left, right))
 
 
 def backward(
@@ -235,12 +254,13 @@
                 out_ref[slot, k] = parts[k]
 
 
-def add_pair(core_ref, mine_ref, others_ref, out_ref):
-    other = others_ref[1 - core_ref[0]]
-    out_ref[...] = (mine_ref[...].astype(F32) + other.astype(F32)).astype(BF16)
-
-
-def filter_gradient(side_ref, features_ref, gathered_ref, out_ref, grad_ref, rows_ref):
+def add_pair(mine_ref, other_ref, out_ref):
+    out_ref[...] = (mine_ref[...].astype(F32) + other_ref[...].astype(F32)).astype(BF16)
+
+
+def filter_gradient(
+    side_ref, features_ref, gathered_ref, act_ref, out_ref, grad_ref, rows_ref
+):
     rows_y, width_in, _ = features_ref.shape
     width_out = grad_ref.shape[0] // 9
     z = lane((width_out, LANES)) % SZ
@@ -276,7 +296,7 @@
         ones, grad_ref[middle : middle + width_out], over_voxels, preferred_element_type=F32
     )
     count = total.shape[0]
-    rounded = total.astype(BF16)
+    rounded = total
     out_ref[:count] = rounded[:, : 2 * width_in]
     last = rounded[:, 2 * width_in :]
     out_ref[count : count + count // 2] = jnp.concatenate(
@@ -293,22 +313,24 @@
         high.astype(F32),
         jnp.where(row == 1, mid.astype(F32), jnp.where(row == 2, low.astype(F32), nothing)),
     ).astype(BF16)
-    out_ref[count + count // 2 :] = jnp.concatenate(
-        [terms, jnp.zeros((16, LANES - width_out), BF16)], axis=1
-    )
+    start = count + count // 2
+    out_ref[start : start + 16] = jnp.concatenate(
+        [terms.astype(F32), jnp.zeros((16, LANES - width_out), F32)], axis=1
+    )
+    out_ref[start + 16 :] = act_ref[1].reshape(2 * width_out, LANES).astype(F32)
 
 
 def finish(
-    side_ref, shares_ref, own_ref, other_ref, sums_ref, theirs_ref, bias_vector_ref,
-    input_ref, weight_ref, bias_ref, act_ref,
+    side_ref, shares_ref, own_ref, other_ref, acted_ref, input_ref, weight_ref, bias_ref, act_ref
 ):
     total = shares_ref[0].astype(F32)
     for k in range(1, shares_ref.shape[0]):
         total = total + shares_ref[k].astype(F32)
     input_ref[...] = total
-    bias = jnp.broadcast_to(bias_vector_ref[...], sums_ref.shape[1:])
-    for k, pre in enumerate(preactivation(side_ref[0], sums_ref, theirs_ref, bias)):
-        act_ref[k] = (0.5 * pre * (1.0 + bend(pre))).astype(BF16)
+    side = side_ref[0]
+    act_ref[pl.ds(2 * side, 2)] = acted_ref[0]
+    received = other_ref[other_ref.shape[0] - 2 * acted_ref.shape[2] :]
+    act_ref[pl.ds(2 - 2 * side, 2)] = received.reshape(acted_ref.shape[1:]).astype(BF16)
     _, width_out, width_in = weight_ref.shape
     count = 9 * width_out
     half = count // 2
@@ -327,8 +349,8 @@
                 piece = both[count + start : count + start + 16, width_in:]
             weight_ref[18 + bc, step : step + 16] = piece
     first = count + half
-    mine = own_ref[first:].astype(F32)
-    theirs = other_ref[first:].astype(F32)
+    mine = own_ref[first : first + 16].astype(F32)
+    theirs = other_ref[first : first + 16].astype(F32)
     bias_ref[...] = (
         jnp.sum(mine, axis=0, keepdims=True) + jnp.sum(theirs, axis=0, keepdims=True)
     )[:, :width_out]
@@ -347,54 +369,47 @@
     work = 2 * 27 * rows_y * LANES * width_in * width_out
     size = rows_y * LANES * 2
 
-    block = 5 * width_out
-    partial = call(
+    cotangent_other = lax.ppermute(cotangent, "sp", swap)
+    block = (2 * n_ci, 2 * width_out + width_out // 2, LANES)
+    partial, bias_columns = call(
         forward,
-        pltpu.VMEM((n_ci, block, LANES), BF16),
-        [SMEM, HBM, HBM],
+        (pltpu.VMEM(block, BF16), pltpu.VMEM((width_out, LANES), F32)),
+        [SMEM, HBM, HBM, HBM],
         work,
         size * (width_in + width_out),
         [
             pltpu.VMEM(features.shape, BF16),
             pltpu.VMEM(taps.shape, BF16),
+            pltpu.VMEM((1, width_out), F32),
             pltpu.VMEM((rows_y + 2, 3 * width_in, LANES), BF16),
             pltpu.VMEM((3 * width_out, 9 * width_in), BF16),
             pltpu.VMEM((3 * width_out, 3 * width_in), BF16),
             pltpu.VMEM((rows_y // 4 + 2, width_in, LANES), BF16),
-            pltpu.SemaphoreType.DMA((2,)),
+            pltpu.SemaphoreType.DMA((3,)),
         ],
-    )(side, stay(features, pltpu.HBM), stay(taps, pltpu.HBM))
-    shares = lax.all_to_all(partial, "ci", 0, 0, tiled=True)
-    own, mine = call(
-        reduce_rows,
-        (shape(cotangent.shape, F32), shape((3, width_out, LANES), F32)),
-        [SMEM, VMEM, VMEM],
+    )(side, *(stay(x, pltpu.HBM) for x in (features, taps, bias_vector.reshape(1, width_out))))
+    both = ("ci", "sp")
+    partial, cotangent_other = lax.optimization_barrier((partial, cotangent_other))
+    shares = lax.all_to_all(partial, both, 0, 0, tiled=True)
+    acted, copies = call(
+        pointwise,
+        (pltpu.VMEM((2, 2, width_out, LANES), BF16), pltpu.VMEM(block, BF16)),
+        [SMEM, VMEM, VMEM, VMEM, VMEM],
         0,
         2 * size * width_out,
-    )(side, shares, cotangent)
-    theirs = lax.ppermute(mine, "sp", swap)
-    bias_column = bias_vector.reshape(width_out, 1)
-    copies = call(
-        pointwise,
-        pltpu.VMEM((n_ci, block, LANES), BF16),
-        [SMEM, VMEM, VMEM, VMEM, VMEM, VMEM],
-        0,
-        2 * size * width_out,
-    )(side, own, mine, theirs, bias_column, cotangent)
-    gathered = lax.all_to_all(copies, "ci", 0, 0, tiled=True)
+    )(side, shares, bias_columns, cotangent, cotangent_other)
+    gathered = lax.all_to_all(copies, both, 0, 0, tiled=True)
     packed = call(
         filter_gradient,
-        shape((9 * width_out + 9 * width_out // 2 + 16, LANES), BF16),
-        [SMEM, VMEM, VMEM],
+        shape((9 * width_out + 9 * width_out // 2 + 16 + 2 * width_out, LANES), F32),
+        [SMEM, VMEM, VMEM, VMEM],
         work,
         size * (width_in + width_out),
         [
             pltpu.VMEM((9 * width_out, rows_y * LANES), BF16),
             pltpu.VMEM((3 * width_in, rows_y * LANES), BF16),
         ],
-    )(side, features, gathered)
-    other = lax.ppermute(packed, "sp", swap)
-    gathered, packed = lax.optimization_barrier((gathered, packed))
+    )(side, features, gathered, acted)
     quarter = (n_co // 2, rows_y // n_co, width_in, LANES)
     mine, other_half = call(
         backward,
@@ -407,14 +422,14 @@
             pltpu.VMEM((3 * width_in, 9 * width_out), BF16),
         ],
     )(side, core, gathered, taps)
-    pairs = [[k, k + 1] for k in range(0, n_co, 2)]
-    halves = lax.all_gather(other_half, "co", axis=0, axis_index_groups=pairs)
+    received = lax.ppermute(other_half, "co", [(k, k ^ 1) for k in range(n_co)])
+    received, packed = lax.optimization_barrier((received, packed))
     summed = call(
-        add_pair, pltpu.VMEM(quarter, BF16), [SMEM, VMEM, VMEM], 0, size * width_in
-    )(core, mine, halves)
-    summed, other = lax.optimization_barrier((summed, other))
+        add_pair, pltpu.VMEM(quarter, BF16), [VMEM, VMEM], 0, size * width_in
+    )(mine, received)
     same_core = [list(range(k, n_co, 2)) for k in range(2)]
     shares = lax.all_to_all(summed, "co", 0, 0, tiled=True, axis_index_groups=same_core)
+    other = lax.ppermute(packed, "sp", swap)
     input_grad, weight_grad, bias_grad, activated = call(
         finish,
         (
@@ -423,10 +438,10 @@
             shape((1, width_out), F32),
             shape(cotangent.shape, BF16),
         ),
-        [SMEM] + [VMEM] * 6,
+        [SMEM] + [VMEM] * 4,
         0,
         27 * 4 * width_in * width_out,
-    )(side, shares, packed, other, own, theirs, bias_column)
+    )(side, shares, packed, other, acted)
     return (activated, input_grad, weight_grad.transpose(0, 2, 1), bias_grad.reshape(width_out))
 
 

time: 66.3 us -> 61.9 us (0.934)
  blocking collectives: 53.9 us -> 47.4 us
  starting transfers between devices: 2.57 us -> 6.55 us
  waiting for transfers between devices: 1.66 us -> 0.01 us
    all_gather x1 -> x0, blocking collectives: 6.46 us -> none  [local(): halves = lax.all_gather(other_half, 'co', axis=0, axis_index_groups=pairs)]
    ppermute x1 -> x2, starting transfers between devices: 1.28 us -> 6.24 us  [the longest x1 4.11 us: local(): received = lax.ppermute(other_half, 'co', [(k, k ^ 1) for k in range(n_co)])]
    ppermute x1 -> x2, waiting for transfers between devices: 1.66 us -> 0.01 us  [the longest x1 0.01 us: local(): cotangent_other = lax.ppermute(cotangent, 'sp', swap)]
    ppermute x1, starting transfers between devices: 1.29 us -> 0.31 us  [local(): other = lax.ppermute(packed, 'sp', swap)]
    pallas_call x5 -> x4, Pallas kernels: 4.74 us -> 4.72 us  [the longest x1 2.57 us: local(): call(forward, (pltpu.VMEM(block, BF16), pltpu.VMEM((width_out, LANES), F3...]
  transfers between devices with their start and end apart: 2 -> 3, of which waited for: 1 -> 0; matrix products, arithmetic and copies ran while one was open for 0% -> 0% of each run, Pallas kernels for 2% -> 7%
where the time goes in v3:
time: 61.9 us; the launch traced here: 61.6 us
  blocking collectives  47.4 us (77%)
  Pallas kernels  6.99 us (11%)
  starting transfers between devices  6.55 us (11%)
  between operations  0.69 us (1%)
    all_to_all x1, blocking collectives, local(): shares = lax.all_to_all(partial, both, 0, 0, tiled=True)  19 us
    all_to_all x1, blocking collectives, local(): lax.all_to_all(summed, 'co', 0, 0, tiled=True, axis_index_groups=same_core)  14.3 us
    all_to_all x1, blocking collectives, local(): gathered = lax.all_to_all(copies, both, 0, 0, tiled=True)  14.1 us
    ppermute x1, starting transfers between devices, local(): received = lax.ppermute(other_half, 'co', [(k, k ^ 1) for k in range(n_co)])  4.11 us
    pallas_call x1, Pallas kernels, local(): call(forward, (pltpu.VMEM(block, BF16), pltpu.VMEM((width_out, LANES), F3...  2.57 us
    ppermute x1, starting transfers between devices, local(): cotangent_other = lax.ppermute(cotangent, 'sp', swap)  2.13 us
    pallas_call x1, Pallas kernels, local(): call(filter_gradient, shape((9 * width_out + 9 * width_out // 2 + 16 + 2...  1.89 us
    pallas_call x1, Pallas kernels, local(): call(backward, (pltpu.VMEM(quarter, BF16), pltpu.VMEM(quarter, BF16)), [S...  1.38 us
  transfers between devices with their start and end apart: 3, of which 0 were waited for; matrix products, arithmetic and copies ran while one was open for 0% of the time, Pallas kernels for 7%

profile of v3, /device:TPU:1, one launch (start us, length us, event | category | flops | bytes accessed | tf_op | source)
XLA Modules:
  0.0 61.6 jit_solution(17429874636349285827)
XLA Ops:
  0.6 2.1 %collective-permute-start = (bf16[4,32,128]{2,1,0:T(8,128)(2,1)}, bf16[4,32,128]{2,1,0:T(8,128)(2,1)S(1)}, u32[]{:S(2)}, u32[]{:S(2)}) collective-permute-start(bf16[4,32,128]{2,1,0:T(8,128)(2,1)} %own_ref.1), channel_id=1, source_target_pairs={{0,1},{1,0},{2,3},{3,2},{4,5},{5,4},{6,7},{7,6},{8,9},{9,8},{10,11... | collective-permute-start | bytes 98312 | tf_op jit(solution)/shard_map/ppermute | solution.py:372
  2.8 2.6 %shard_map.75 = (bf16[16,80,128]{2,1,0:T(8,128)(2,1)S(1)}, f32[32,128]{1,0:T(8,128)S(1)}) custom-call(s32[1]{0:T(128)} %bitcast.side_ref, bf16[32,64,128]{2,1,0:T(8,128)(2,1)} %features_ref.1, bf16[27,32,64]{2,1,0:T(8,128)(2,1)} %bitcast.6, f32[1,32]{1,0:T(1,128)} %bitcast.9), custom_call_target="tpu_custom_call" | custom-call | flops 452984832 | bytes 786432 | tf_op jit(solution)/shard_map/pallas_call | solution.py:374
  5.3 0.0 collective-permute-done.other_ref
  5.3 0.0 copy-start
  5.4 19.0 %all_to_all.15.shares_ref = bf16[16,80,128]{2,1,0:T(8,128)(2,1)S(1)} all-to-all(bf16[16,80,128]{2,1,0:T(8,128)(2,1)S(1)} %get-tuple-element.23), channel_id=1, replica_groups=mesh['ci'=8,'co'=16,'sp'=2] {'ci','sp'}, dimensions={0} | all-to-all | bytes 655360 | tf_op jit(solution)/shard_map/all_to_all | solution.py:393
  24.4 0.0 copy-done
  24.4 0.2 shard_map.76
  24.6 0.0 copy-start.2
  24.6 14.1 %all_to_all.16.gathered_ref = bf16[16,80,128]{2,1,0:T(8,128)(2,1)S(1)} all-to-all(bf16[16,80,128]{2,1,0:T(8,128)(2,1)S(1)} %get-tuple-element.26), channel_id=1, replica_groups=mesh['ci'=8,'co'=16,'sp'=2] {'ci','sp'}, dimensions={0} | all-to-all | bytes 655360 | tf_op jit(solution)/shard_map/all_to_all | solution.py:401
  38.7 0.0 copy-done.2
  38.7 0.0 copy-start.1
  38.7 1.4 %shard_map.77 = (bf16[8,2,64,128]{3,2,1,0:T(8,128)(2,1)S(1)}, bf16[8,2,64,128]{3,2,1,0:T(8,128)(2,1)S(1)}) custom-call(s32[1]{0:T(128)} %bitcast.side_ref, s32[1]{0:T(128)} %bitcast.1.core_ref, bf16[16,80,128]{2,1,0:T(8,128)(2,1)S(1)} %all_to_all.16.gathered_ref, bf16[27,32,64]{2,1,0:T(8,128)(2,1)S(1)} %bitcast.7), custom_call_target="tpu_custom_call" | custom-call | flops 452984832 | bytes 786432 | tf_op jit(solution)/shard_map/pallas_call | solution.py:414
  40.1 4.1 %collective-permute-start.1 = (bf16[8,2,64,128]{3,2,1,0:T(8,128)(2,1)S(1)}, bf16[8,2,64,128]{3,2,1,0:T(8,128)(2,1)S(1)}, u32[]{:S(2)}, u32[]{:S(2)}) collective-permute-start(bf16[8,2,64,128]{3,2,1,0:T(8,128)(2,1)S(1)} %get-tuple-element.28), channel_id=1, source_target_pairs={{0,2},{2,0},{4,6},{6,4},{8,10},{10,8},{12,14},{14,12},{16,18},{18,... | collective-permute-start | bytes 786440 | tf_op jit(solution)/shard_map/ppermute | solution.py:425
  44.2 0.0 copy-done.1
  44.2 1.9 %shard_map.78.own_ref = f32[512,128]{1,0:T(8,128)S(1)} custom-call(s32[1]{0:T(128)} %bitcast.side_ref, bf16[32,64,128]{2,1,0:T(8,128)(2,1)S(1)} %copy-done.1, bf16[16,80,128]{2,1,0:T(8,128)(2,1)S(1)} %all_to_all.16.gathered_ref, bf16[2,2,32,128]{3,2,1,0:T(8,128)(2,1)S(1)} %get-tuple-element.29.act_ref.acted_ref), custom_call_target="tpu_custom_call" | custom-call | flops 452984832 | bytes 786432 | tf_op jit(solution)/shard_map/pallas_call | solution.py:402
  46.1 0.0 collective-permute-done.1.other_ref
  46.1 0.3 collective-permute-start.2
  46.4 0.1 shard_map.79
  46.5 14.3 %all_to_all.17.shares_ref = bf16[8,2,64,128]{3,2,1,0:T(8,128)(2,1)S(1)} all-to-all(bf16[8,2,64,128]{3,2,1,0:T(8,128)(2,1)S(1)} %shard_map.79), channel_id=1, replica_groups={{0,4,8,12,16,20,24,28},{2,6,10,14,18,22,26,30},{1,5,9,13,17,21,25,29},{..., dimensions={0} | all-to-all | bytes 524288 | tf_op jit(solution)/shard_map/all_to_all | solution.py:431
  60.7 0.0 collective-permute-done.2.other_ref
  60.7 0.9 %shard_map.80 = (f32[2,64,128]{2,1,0:T(8,128)}, f32[27,32,64]{2,1,0:T(8,128)}, f32[1,32]{1,0:T(1,128)}, bf16[4,32,128]{2,1,0:T(8,128)(2,1)}) custom-call(s32[1]{0:T(128)} %bitcast.side_ref, bf16[8,2,64,128]{3,2,1,0:T(8,128)(2,1)S(1)} %all_to_all.17.shares_ref, f32[512,128]{1,0:T(8,128)S(1)} %shard_map.78.own_ref, ...), custom_call_target="tpu_custom_call" | custom-call | bytes 221184 | tf_op jit(solution)/shard_map/pallas_call | solution.py:433
Async XLA Ops:
  0.6 4.7 %collective-permute-start = (bf16[4,32,128]{2,1,0:T(8,128)(2,1)}, bf16[4,32,128]{2,1,0:T(8,128)(2,1)S(1)}, u32[]{:S(2)}, u32[]{:S(2)}) collective-permute-start(bf16[4,32,128]{2,1,0:T(8,128)(2,1)} %own_ref.1), channel_id=1, source_target_pairs={{0,1},{1,0},{2,3},{3,2},{4,5},{5,4},{6,7},{7,6},{8,9},{9,8},{10,11... | collective-permute-start | bytes 98312 | tf_op jit(solution)/shard_map/ppermute | solution.py:372
  5.3 19.0 %copy-start = (bf16[4,32,128]{2,1,0:T(8,128)(2,1)S(1)}, bf16[4,32,128]{2,1,0:T(8,128)(2,1)}, u32[]{:S(2)}) copy-start(bf16[4,32,128]{2,1,0:T(8,128)(2,1)} %own_ref.1) | copy-start | bytes 98308
  24.6 14.1 %copy-start.2 = (bf16[27,64,32]{1,2,0:T(8,128)(2,1)S(1)}, bf16[27,64,32]{1,2,0:T(8,128)(2,1)}, u32[]{:S(2)}) copy-start(bf16[27,64,32]{1,2,0:T(8,128)(2,1)} %param.5) | copy-start | bytes 331780
  38.7 5.5 %copy-start.1 = (bf16[32,64,128]{2,1,0:T(8,128)(2,1)S(1)}, bf16[32,64,128]{2,1,0:T(8,128)(2,1)}, u32[]{:S(2)}) copy-start(bf16[32,64,128]{2,1,0:T(8,128)(2,1)} %features_ref.1) | copy-start | bytes 1572868
  40.1 6.0 %collective-permute-start.1 = (bf16[8,2,64,128]{3,2,1,0:T(8,128)(2,1)S(1)}, bf16[8,2,64,128]{3,2,1,0:T(8,128)(2,1)S(1)}, u32[]{:S(2)}, u32[]{:S(2)}) collective-permute-start(bf16[8,2,64,128]{3,2,1,0:T(8,128)(2,1)S(1)} %get-tuple-element.28), channel_id=1, source_target_pairs={{0,2},{2,0},{4,6},{6,4},{8,10},{10,8},{12,14},{14,12},{16,18},{18,... | collective-permute-start | bytes 786440 | tf_op jit(solution)/shard_map/ppermute | solution.py:425
  46.1 14.6 %collective-permute-start.2 = (f32[512,128]{1,0:T(8,128)S(1)}, f32[512,128]{1,0:T(8,128)S(1)}, u32[]{:S(2)}, u32[]{:S(2)}) collective-permute-start(f32[512,128]{1,0:T(8,128)S(1)} %shard_map.78.own_ref), channel_id=1, source_target_pairs={{0,1},{1,0},{2,3},{3,2},{4,5},{5,4},{6,7},{7,6},{8,9},{9,8},{10,11... | collective-permute-start | bytes 786440 | tf_op jit(solution)/shard_map/ppermute | solution.py:432

commit v4 on v3

--- a/solution.py
+++ b/solution.py
@@ -40,13 +40,11 @@
     return packed
 
 
-def neighbours(own, left=None, right=None):
+def neighbours(own):
     at = lane(own.shape)
     zero = jnp.zeros_like(own)
-    before = jnp.where(at < SZ, zero if left is None else left, pltpu.roll(own, SZ, 1))
-    after = jnp.where(
-        at >= LANES - SZ, zero if right is None else right, pltpu.roll(own, LANES - SZ, 1)
-    )
+    before = jnp.where(at < SZ, zero, pltpu.roll(own, SZ, 1))
+    after = jnp.where(at >= LANES - SZ, zero, pltpu.roll(own, LANES - SZ, 1))
     return before, own, after
 
 
@@ -64,7 +62,7 @@
     for k in range(4):
         h, row = divmod(k, 2)
         piece = rows[row][h * half : (h + 1) * half]
-        moved = pltpu.roll(piece, (SZ * k - source) % LANES, 1)
+        moved = pltpu.roll(piece, lax.rem(SZ * k - source + LANES, LANES), 1)
         packed = moved if k == 0 else jnp.where(at >= SZ * k, moved, packed)
     return packed
 
@@ -214,21 +212,8 @@
         out_ref[k] = blocks[k % 2]
 
 
-def spread_gradient(side, gathered_ref, width, put):
-    for slot in range(gathered_ref.shape[0]):
-        packed = gathered_ref[slot, 2 * width :]
-        zero = jnp.zeros_like(packed)
-        low = jnp.where(side == 1, packed, zero)
-        high = jnp.where(side == 0, packed, zero)
-        for row in range(2):
-            own = gathered_ref[slot, row * width : (row + 1) * width]
-            left = unpack_row(low, row, 0)
-            right = unpack_row(high, row, LANES - SZ)
-            put(2 * slot + row, neighbours(own, left, right))
-
-
 def backward(
-    side_ref, core_ref, gathered_ref, weight_ref, mine_ref, other_ref, spread_ref, taps_ref
+    side_ref, core_ref, gathered_ref, weight_ref, mine_ref, other_ref, spread_ref, taps_ref,
 ):
     slots, rows, width_in, _ = mine_ref.shape
     rows_y = 2 * slots * rows
@@ -238,11 +223,34 @@
     spread_ref[0] = blank
     spread_ref[rows_y + 1] = blank
 
-    def put(y, seen):
-        for b in range(3):
-            spread_ref[y + 1, b * width_out : (b + 1) * width_out] = seen[b]
-
-    spread_gradient(side_ref[0], gathered_ref, width_out, put)
+    side = side_ref[0]
+    half, at = width_out // 2, lane((width_out, LANES))
+    target = (LANES - SZ) * (1 - side)
+    for slot in range(gathered_ref.shape[0]):
+        packed = gathered_ref[slot, 2 * width_out :]
+        for row in range(2):
+            beside = jnp.concatenate(
+                [
+                    pltpu.roll(packed, lax.rem(target + 2 * LANES - SZ * (2 * h + row), LANES), 1)
+                    for h in range(2)
+                ],
+                axis=0,
+            )
+            zero = jnp.zeros_like(beside)
+            own = gathered_ref[slot, row * width_out : (row + 1) * width_out]
+            seen = (
+                jnp.where(
+                    at < SZ, jnp.where(side == 1, beside, zero), pltpu.roll(own, SZ, 1)
+                ),
+                own,
+                jnp.where(
+                    at >= LANES - SZ,
+                    jnp.where(side == 0, beside, zero),
+                    pltpu.roll(own, LANES - SZ, 1),
+                ),
+            )
+            for b in range(3):
+                spread_ref[2 * slot + row + 1, b * width_out : (b + 1) * width_out] = seen[b]
     for c in range(3):
         block = jnp.concatenate([weight_ref[26 - 3 * ab - c] for ab in range(9)], axis=0)
         taps_ref[c * width_in : (c + 1) * width_in] = block.T
@@ -258,66 +266,41 @@
     out_ref[...] = (mine_ref[...].astype(F32) + other_ref[...].astype(F32)).astype(BF16)
 
 
-def filter_gradient(
-    side_ref, features_ref, gathered_ref, act_ref, out_ref, grad_ref, rows_ref
-):
+def filter_gradient(features_ref, spread_ref, act_ref, out_ref, grad_ref, rows_ref):
     rows_y, width_in, _ = features_ref.shape
-    width_out = grad_ref.shape[0] // 9
-    z = lane((width_out, LANES)) % SZ
-    zero = jnp.zeros((width_out, LANES), BF16)
-
-    def put(y, seen):
+    third = spread_ref.shape[1]
+    width = third // 3
+    z = lane((third, LANES)) % SZ
+    zero = jnp.zeros((third, LANES), BF16)
+    for y in range(rows_y):
+        own = spread_ref[y + 1]
+        moved = (
+            jnp.where(z == SZ - 1, zero, pltpu.roll(own, LANES - 1, 1)),
+            own,
+            jnp.where(z == 0, zero, pltpu.roll(own, 1, 1)),
+        )
         columns = slice(y * LANES, (y + 1) * LANES)
-        for b in range(3):
-            own = seen[2 - b]
-            moved = (
-                jnp.where(z == SZ - 1, zero, pltpu.roll(own, LANES - 1, 1)),
-                own,
-                jnp.where(z == 0, zero, pltpu.roll(own, 1, 1)),
-            )
-            for c in range(3):
-                start = (3 * b + c) * width_out
-                grad_ref[start : start + width_out, columns] = moved[c]
-
-    spread_gradient(side_ref[0], gathered_ref, width_out, put)
-    for a in range(3):
-        for y in range(rows_y):
+        for c in range(3):
+            grad_ref[c * third : (c + 1) * third, columns] = moved[c]
+        for a in range(3):
             source = y + a - 1
             inside = 0 <= source < rows_y
-            rows_ref[a * width_in : (a + 1) * width_in, y * LANES : (y + 1) * LANES] = (
+            rows_ref[a * width_in : (a + 1) * width_in, columns] = (
                 features_ref[source] if inside else jnp.zeros((width_in, LANES), BF16)
             )
-    over_voxels = (((1,), (1,)), ((), ()))
-    grads = grad_ref[...]
-    total = lax.dot_general(grads, rows_ref[...], over_voxels, preferred_element_type=F32)
-    middle = 4 * width_out
-    ones = jnp.ones((16, grads.shape[1]), BF16)
-    bias = lax.dot_general(
-        ones, grad_ref[middle : middle + width_out], over_voxels, preferred_element_type=F32
+        rows_ref[3 * width_in :, columns] = jnp.ones((16, LANES), BF16)
+    total = lax.dot_general(
+        grad_ref[...], rows_ref[...], (((1,), (1,)), ((), ())), preferred_element_type=F32
     )
     count = total.shape[0]
-    rounded = total
-    out_ref[:count] = rounded[:, : 2 * width_in]
-    last = rounded[:, 2 * width_in :]
-    out_ref[count : count + count // 2] = jnp.concatenate(
-        [last[: count // 2], last[count // 2 :]], axis=1
-    )
-    high = bias.astype(BF16)
-    rest = bias - high.astype(F32)
-    mid = rest.astype(BF16)
-    low = (rest - mid.astype(F32)).astype(BF16)
-    row = lax.broadcasted_iota(jnp.int32, bias.shape, 0)
-    nothing = jnp.zeros_like(bias)
-    terms = jnp.where(
-        row == 0,
-        high.astype(F32),
-        jnp.where(row == 1, mid.astype(F32), jnp.where(row == 2, low.astype(F32), nothing)),
-    ).astype(BF16)
-    start = count + count // 2
-    out_ref[start : start + 16] = jnp.concatenate(
-        [terms.astype(F32), jnp.zeros((16, LANES - width_out), F32)], axis=1
-    )
-    out_ref[start + 16 :] = act_ref[1].reshape(2 * width_out, LANES).astype(F32)
+    half = count // 2
+    out_ref[:count] = total[:, : 2 * width_in]
+    last = total[:, 2 * width_in : 3 * width_in]
+    out_ref[count : count + half] = jnp.concatenate([last[:half], last[half:]], axis=1)
+    start = count + half
+    bias = total[third + width : third + 2 * width, 3 * width_in : 3 * width_in + 1]
+    out_ref[start : start + width] = jnp.broadcast_to(bias, (width, LANES))
+    out_ref[start + width :] = act_ref[1].reshape(2 * width, LANES).astype(F32)
 
 
 def finish(
@@ -334,26 +317,24 @@
     _, width_out, width_in = weight_ref.shape
     count = 9 * width_out
     half = count // 2
-    both = own_ref[...].astype(F32) + other_ref[...].astype(F32)
-    for bc in range(9):
-        rows = slice(bc * width_out, (bc + 1) * width_out)
-        first = both[rows]
-        weight_ref[bc] = first[:, :width_in]
-        weight_ref[9 + bc] = first[:, width_in:]
-        for step in range(0, width_out, 16):
-            start = bc * width_out + step
-            if start < half:
-                piece = both[count + start : count + start + 16, :width_in]
-            else:
-                start -= half
-                piece = both[count + start : count + start + 16, width_in:]
-            weight_ref[18 + bc, step : step + 16] = piece
-    first = count + half
-    mine = own_ref[first : first + 16].astype(F32)
-    theirs = other_ref[first : first + 16].astype(F32)
-    bias_ref[...] = (
-        jnp.sum(mine, axis=0, keepdims=True) + jnp.sum(theirs, axis=0, keepdims=True)
-    )[:, :width_out]
+    both = own_ref[: count + half + width_out] + other_ref[: count + half + width_out]
+    for b in range(3):
+        for c in range(3):
+            start = (3 * c + 2 - b) * width_out
+            first = both[start : start + width_out]
+            weight_ref[3 * b + c] = first[:, :width_in]
+            weight_ref[9 + 3 * b + c] = first[:, width_in:]
+            for step in range(0, width_out, 16):
+                row = start + step
+                if row < half:
+                    piece = both[count + row : count + row + 16, :width_in]
+                else:
+                    piece = both[half + row : half + row + 16, width_in:]
+                weight_ref[18 + 3 * b + c, step : step + 16] = piece
+    shape = (width_out, width_out)
+    diagonal = lax.broadcasted_iota(jnp.int32, shape, 0) == lane(shape)
+    sums = both[count + half :, :width_out]
+    bias_ref[...] = jnp.sum(jnp.where(diagonal, sums, 0.0), axis=0, keepdims=True)
 
 
 def local(features, weight, bias_vector, cotangent):
@@ -399,29 +380,30 @@
         2 * size * width_out,
     )(side, shares, bias_columns, cotangent, cotangent_other)
     gathered = lax.all_to_all(copies, both, 0, 0, tiled=True)
+    quarter = (n_co // 2, rows_y // n_co, width_in, LANES)
+    mine, other_half, spread = call(
+        backward,
+        (
+            pltpu.VMEM(quarter, BF16),
+            pltpu.VMEM(quarter, BF16),
+            pltpu.VMEM((rows_y + 2, 3 * width_out, LANES), BF16),
+        ),
+        [SMEM, SMEM, VMEM, VMEM],
+        work,
+        size * (width_in + width_out),
+        [pltpu.VMEM((3 * width_in, 9 * width_out), BF16)],
+    )(side, core, gathered, taps)
     packed = call(
         filter_gradient,
-        shape((9 * width_out + 9 * width_out // 2 + 16 + 2 * width_out, LANES), F32),
-        [SMEM, VMEM, VMEM, VMEM],
+        shape((9 * width_out + 9 * width_out // 2 + 3 * width_out, LANES), F32),
+        [VMEM, VMEM, VMEM],
         work,
         size * (width_in + width_out),
         [
             pltpu.VMEM((9 * width_out, rows_y * LANES), BF16),
-            pltpu.VMEM((3 * width_in, rows_y * LANES), BF16),
+            pltpu.VMEM((3 * width_in + 16, rows_y * LANES), BF16),
         ],
-    )(side, features, gathered, acted)
-    quarter = (n_co // 2, rows_y // n_co, width_in, LANES)
-    mine, other_half = call(
-        backward,
-        (pltpu.VMEM(quarter, BF16), pltpu.VMEM(quarter, BF16)),
-        [SMEM, SMEM, VMEM, VMEM],
-        work,
-        size * (width_in + width_out),
-        [
-            pltpu.VMEM((rows_y + 2, 3 * width_out, LANES), BF16),
-            pltpu.VMEM((3 * width_in, 9 * width_out), BF16),
-        ],
-    )(side, core, gathered, taps)
+    )(features, spread, acted)
     received = lax.ppermute(other_half, "co", [(k, k ^ 1) for k in range(n_co)])
     received, packed = lax.optimization_barrier((received, packed))
     summed = call(

time: 61.9 us -> 60.7 us (0.981)
  Pallas kernels: 6.99 us -> 6.07 us
    pallas_call x2, Pallas kernels: 3.27 us -> 2.35 us  [the longest x1 1.35 us: local(): call(backward, (pltpu.VMEM(quarter, BF16), pltpu.VMEM(quarter, BF16), plt...]
  transfers between devices with their start and end apart: 3 -> 3, of which waited for: 0 -> 1; matrix products, arithmetic and copies ran while one was open for 0% -> 0% of each run, Pallas kernels for 7% -> 6%
where the time goes in v4:
time: 60.7 us; the launch traced here: 60.4 us
  blocking collectives  47 us (77%)
  starting transfers between devices  6.47 us (11%)
  Pallas kernels  6.07 us (10%)
  between operations  0.68 us (1%)
    all_to_all x1, blocking collectives, local(): shares = lax.all_to_all(partial, both, 0, 0, tiled=True)  19 us
    all_to_all x1, blocking collectives, local(): gathered = lax.all_to_all(copies, both, 0, 0, tiled=True)  14.1 us
    all_to_all x1, blocking collectives, local(): lax.all_to_all(summed, 'co', 0, 0, tiled=True, axis_index_groups=same_core)  13.9 us
    ppermute x1, starting transfers between devices, local(): received = lax.ppermute(other_half, 'co', [(k, k ^ 1) for k in range(n_co)])  4.12 us
    pallas_call x1, Pallas kernels, local(): call(forward, (pltpu.VMEM(block, BF16), pltpu.VMEM((width_out, LANES), F3...  2.57 us
    ppermute x1, starting transfers between devices, local(): cotangent_other = lax.ppermute(cotangent, 'sp', swap)  2.13 us
    pallas_call x1, Pallas kernels, local(): call(backward, (pltpu.VMEM(quarter, BF16), pltpu.VMEM(quarter, BF16), plt...  1.35 us
  transfers between devices with their start and end apart: 3, of which 1 were waited for; matrix products, arithmetic and copies ran while one was open for 0% of the time, Pallas kernels for 6%

profile of v4, /device:TPU:1, one launch (start us, length us, event | category | flops | bytes accessed | tf_op | source)
XLA Modules:
  0.0 60.4 jit_solution(7108439958273564401)
XLA Ops:
  0.6 2.1 %collective-permute-start = (bf16[4,32,128]{2,1,0:T(8,128)(2,1)}, bf16[4,32,128]{2,1,0:T(8,128)(2,1)S(1)}, u32[]{:S(2)}, u32[]{:S(2)}) collective-permute-start(bf16[4,32,128]{2,1,0:T(8,128)(2,1)} %own_ref.1), channel_id=1, source_target_pairs={{0,1},{1,0},{2,3},{3,2},{4,5},{5,4},{6,7},{7,6},{8,9},{9,8},{10,11... | collective-permute-start | bytes 98312 | tf_op jit(solution)/shard_map/ppermute | solution.py:353
  2.8 2.6 %shard_map.75 = (bf16[16,80,128]{2,1,0:T(8,128)(2,1)S(1)}, f32[32,128]{1,0:T(8,128)S(1)}) custom-call(s32[1]{0:T(128)} %bitcast.side_ref, bf16[32,64,128]{2,1,0:T(8,128)(2,1)} %features_ref.1, bf16[27,32,64]{2,1,0:T(8,128)(2,1)} %bitcast.6, f32[1,32]{1,0:T(1,128)} %bitcast.9), custom_call_target="tpu_custom_call" | custom-call | flops 452984832 | bytes 786432 | tf_op jit(solution)/shard_map/pallas_call | solution.py:355
  5.3 0.0 collective-permute-done.other_ref
  5.3 0.0 copy-start
  5.4 19.0 %all_to_all.15.shares_ref = bf16[16,80,128]{2,1,0:T(8,128)(2,1)S(1)} all-to-all(bf16[16,80,128]{2,1,0:T(8,128)(2,1)S(1)} %get-tuple-element.24), channel_id=1, replica_groups=mesh['ci'=8,'co'=16,'sp'=2] {'ci','sp'}, dimensions={0} | all-to-all | bytes 655360 | tf_op jit(solution)/shard_map/all_to_all | solution.py:374
  24.4 0.0 copy-done
  24.4 0.2 shard_map.76
  24.6 0.0 copy-start.2
  24.6 14.1 %all_to_all.16.gathered_ref = bf16[16,80,128]{2,1,0:T(8,128)(2,1)S(1)} all-to-all(bf16[16,80,128]{2,1,0:T(8,128)(2,1)S(1)} %get-tuple-element.27), channel_id=1, replica_groups=mesh['ci'=8,'co'=16,'sp'=2] {'ci','sp'}, dimensions={0} | all-to-all | bytes 655360 | tf_op jit(solution)/shard_map/all_to_all | solution.py:382
  38.7 0.0 copy-done.2
  38.7 0.0 copy-start.1
  38.7 1.3 %shard_map.77 = (bf16[8,2,64,128]{3,2,1,0:T(8,128)(2,1)S(1)}, bf16[8,2,64,128]{3,2,1,0:T(8,128)(2,1)S(1)}, bf16[34,96,128]{2,1,0:T(8,128)(2,1)S(1)}) custom-call(s32[1]{0:T(128)} %bitcast.side_ref, s32[1]{0:T(128)} %bitcast.1.core_ref, bf16[16,80,128]{2,1,0:T(8,128)(2,1)S(1)} %all_to_all.16.gathered_ref, bf16[27,32,64]{2,1,0:T(8,128)(2,1)S(1)} %bitcast.7), custom_call_target="tpu_custom_call" | custom-call | flops 452984832 | bytes 786432 | tf_op jit(solution)/shard_map/pallas_call | solution.py:384
  40.0 4.1 %collective-permute-start.1 = (bf16[8,2,64,128]{3,2,1,0:T(8,128)(2,1)S(1)}, bf16[8,2,64,128]{3,2,1,0:T(8,128)(2,1)S(1)}, u32[]{:S(2)}, u32[]{:S(2)}) collective-permute-start(bf16[8,2,64,128]{3,2,1,0:T(8,128)(2,1)S(1)} %get-tuple-element.29), channel_id=1, source_target_pairs={{0,2},{2,0},{4,6},{6,4},{8,10},{10,8},{12,14},{14,12},{16,18},{18,... | collective-permute-start | bytes 786440 | tf_op jit(solution)/shard_map/ppermute | solution.py:407
  44.2 0.0 copy-done.1
  44.2 1.0 %shard_map.78.own_ref = f32[528,128]{1,0:T(8,128)S(1)} custom-call(bf16[32,64,128]{2,1,0:T(8,128)(2,1)S(1)} %copy-done.1, bf16[34,96,128]{2,1,0:T(8,128)(2,1)S(1)} %get-tuple-element.30.spread_ref, bf16[2,2,32,128]{3,2,1,0:T(8,128)(2,1)S(1)} %get-tuple-element.31.act_ref.acted_ref), custom_call_target="tpu_custom_call" | custom-call | flops 452984832 | bytes 786432 | tf_op jit(solution)/shard_map/pallas_call | solution.py:396
  45.2 0.2 collective-permute-done.1.other_ref
  45.3 0.2 collective-permute-start.2
  45.5 0.1 shard_map.79
  45.6 13.9 %all_to_all.17.shares_ref = bf16[8,2,64,128]{3,2,1,0:T(8,128)(2,1)S(1)} all-to-all(bf16[8,2,64,128]{3,2,1,0:T(8,128)(2,1)S(1)} %shard_map.79), channel_id=1, replica_groups={{0,4,8,12,16,20,24,28},{2,6,10,14,18,22,26,30},{1,5,9,13,17,21,25,29},{..., dimensions={0} | all-to-all | bytes 524288 | tf_op jit(solution)/shard_map/all_to_all | solution.py:413
  59.5 0.0 collective-permute-done.2.other_ref
  59.5 0.9 %shard_map.80 = (f32[2,64,128]{2,1,0:T(8,128)}, f32[27,32,64]{2,1,0:T(8,128)}, f32[1,32]{1,0:T(1,128)}, bf16[4,32,128]{2,1,0:T(8,128)(2,1)}) custom-call(s32[1]{0:T(128)} %bitcast.side_ref, bf16[8,2,64,128]{3,2,1,0:T(8,128)(2,1)S(1)} %all_to_all.17.shares_ref, f32[528,128]{1,0:T(8,128)S(1)} %shard_map.78.own_ref, ...), custom_call_target="tpu_custom_call" | custom-call | bytes 221184 | tf_op jit(solution)/shard_map/pallas_call | solution.py:415
Async XLA Ops:
  0.6 4.7 %collective-permute-start = (bf16[4,32,128]{2,1,0:T(8,128)(2,1)}, bf16[4,32,128]{2,1,0:T(8,128)(2,1)S(1)}, u32[]{:S(2)}, u32[]{:S(2)}) collective-permute-start(bf16[4,32,128]{2,1,0:T(8,128)(2,1)} %own_ref.1), channel_id=1, source_target_pairs={{0,1},{1,0},{2,3},{3,2},{4,5},{5,4},{6,7},{7,6},{8,9},{9,8},{10,11... | collective-permute-start | bytes 98312 | tf_op jit(solution)/shard_map/ppermute | solution.py:353
  5.3 19.0 %copy-start = (bf16[4,32,128]{2,1,0:T(8,128)(2,1)S(1)}, bf16[4,32,128]{2,1,0:T(8,128)(2,1)}, u32[]{:S(2)}) copy-start(bf16[4,32,128]{2,1,0:T(8,128)(2,1)} %own_ref.1) | copy-start | bytes 98308
  24.6 14.1 %copy-start.2 = (bf16[27,64,32]{1,2,0:T(8,128)(2,1)S(1)}, bf16[27,64,32]{1,2,0:T(8,128)(2,1)}, u32[]{:S(2)}) copy-start(bf16[27,64,32]{1,2,0:T(8,128)(2,1)} %param.5) | copy-start | bytes 331780
  38.7 5.5 %copy-start.1 = (bf16[32,64,128]{2,1,0:T(8,128)(2,1)S(1)}, bf16[32,64,128]{2,1,0:T(8,128)(2,1)}, u32[]{:S(2)}) copy-start(bf16[32,64,128]{2,1,0:T(8,128)(2,1)} %features_ref.1) | copy-start | bytes 1572868
  40.0 5.3 %collective-permute-start.1 = (bf16[8,2,64,128]{3,2,1,0:T(8,128)(2,1)S(1)}, bf16[8,2,64,128]{3,2,1,0:T(8,128)(2,1)S(1)}, u32[]{:S(2)}, u32[]{:S(2)}) collective-permute-start(bf16[8,2,64,128]{3,2,1,0:T(8,128)(2,1)S(1)} %get-tuple-element.29), channel_id=1, source_target_pairs={{0,2},{2,0},{4,6},{6,4},{8,10},{10,8},{12,14},{14,12},{16,18},{18,... | collective-permute-start | bytes 786440 | tf_op jit(solution)/shard_map/ppermute | solution.py:407
  45.3 14.2 %collective-permute-start.2 = (f32[528,128]{1,0:T(8,128)S(1)}, f32[528,128]{1,0:T(8,128)S(1)}, u32[]{:S(2)}, u32[]{:S(2)}) collective-permute-start(f32[528,128]{1,0:T(8,128)S(1)} %shard_map.78.own_ref), channel_id=1, source_target_pairs={{0,1},{1,0},{2,3},{3,2},{4,5},{5,4},{6,7},{7,6},{8,9},{9,8},{10,11... | collective-permute-start | bytes 811016 | tf_op jit(solution)/shard_map/ppermute | solution.py:414

commit v5 on v4

--- a/solution.py
+++ b/solution.py
@@ -9,6 +9,8 @@
 LANES = 128
 BF16 = jnp.bfloat16
 F32 = jnp.float32
+OVER_CI_SP = [0, 14, 12, 10, 8, 6, 4, 2, 1, 15, 13, 11, 9, 7, 5, 3]
+OVER_CO = [0, 4, 1, 5, 2, 6, 3, 7]
 VMEM = pl.BlockSpec(memory_space=pltpu.VMEM)
 SMEM = pl.BlockSpec(memory_space=pltpu.SMEM)
 HBM = pl.BlockSpec(memory_space=pltpu.HBM)
@@ -85,7 +87,7 @@
 def correlate_rows(taps, spread_ref, y, width):
     depth = 3 * spread_ref.shape[1]
     columns = jnp.concatenate(
-        [spread_ref[pl.ds(y + k, 3)].reshape(depth, LANES) for k in range(2)], axis=1
+        [spread_ref[y + k : y + k + 3].reshape(depth, LANES) for k in range(2)], axis=1
     )
     product = jnp.dot(taps, columns, preferred_element_type=F32)
     parts = along_z([product[c * width : (c + 1) * width] for c in range(3)])
@@ -131,10 +133,11 @@
             for b in range(3):
                 spread_ref[4 * group + k + 1, b * width_in : (b + 1) * width_in] = seen[b]
         edge_ref[group + 1] = pack_plane(side, planes)
-        while done + 2 < 4 * group + 4 or (group == groups - 1 and done < rows_y):
+        while done + 2 < 4 * group or (group == groups - 1 and done < rows_y):
             parts = correlate_rows(taps, spread_ref, done, width_out)
             for k in range(2):
-                out_ref[done // 2, k * width_out : (k + 1) * width_out] = parts[k]
+                place = OVER_CI_SP.index(done // 2)
+                out_ref[place, k * width_out : (k + 1) * width_out] = parts[k]
             done += 2
     none = jnp.zeros(edge_ref.shape[1:], BF16)
     edge_ref[0] = none
@@ -161,8 +164,9 @@
         turned = pltpu.roll(here, LANES // 2, 1)
         first = jnp.where(low, here[:half], turned[half:])
         second = jnp.where(low, turned[:half], here[half:])
-        out_ref[2 * group, 2 * width_out :] = first.astype(BF16)
-        out_ref[2 * group + 1, 2 * width_out :] = second.astype(BF16)
+        for k, part in enumerate((first, second)):
+            place = OVER_CI_SP.index(2 * group + k)
+            out_ref[place, 2 * width_out :] = part.astype(BF16)
 
 
 def bend(pre):
@@ -183,8 +187,9 @@
     bias = bias_ref[...]
     sums = []
     for h in range(2):
-        total = shares_ref[h].astype(F32)
-        for k in range(2 + h, shares_ref.shape[0], 2):
+        places = [k for k, owner in enumerate(OVER_CI_SP) if owner % 2 == h]
+        total = shares_ref[places[0]].astype(F32)
+        for k in places[1:]:
             total = total + shares_ref[k].astype(F32)
         sums.append(total)
     at = lane((width, LANES))
@@ -209,7 +214,7 @@
         for h in range(2)
     ]
     for k in range(out_ref.shape[0]):
-        out_ref[k] = blocks[k % 2]
+        out_ref[k] = blocks[OVER_CI_SP[k] % 2]
 
 
 def backward(
@@ -223,11 +228,17 @@
     spread_ref[0] = blank
     spread_ref[rows_y + 1] = blank
 
+    for c in range(3):
+        block = jnp.concatenate([weight_ref[26 - 3 * ab - c] for ab in range(9)], axis=0)
+        taps_ref[c * width_in : (c + 1) * width_in] = block.T
+    taps = taps_ref[...]
     side = side_ref[0]
     half, at = width_out // 2, lane((width_out, LANES))
     target = (LANES - SZ) * (1 - side)
-    for slot in range(gathered_ref.shape[0]):
-        packed = gathered_ref[slot, 2 * width_out :]
+    done = 0
+    for slot in range(2 * slots):
+        place = OVER_CI_SP.index(slot)
+        packed = gathered_ref[place, 2 * width_out :]
         for row in range(2):
             beside = jnp.concatenate(
                 [
@@ -237,7 +248,7 @@
                 axis=0,
             )
             zero = jnp.zeros_like(beside)
-            own = gathered_ref[slot, row * width_out : (row + 1) * width_out]
+            own = gathered_ref[place, row * width_out : (row + 1) * width_out]
             seen = (
                 jnp.where(
                     at < SZ, jnp.where(side == 1, beside, zero), pltpu.roll(own, SZ, 1)
@@ -251,15 +262,13 @@
             )
             for b in range(3):
                 spread_ref[2 * slot + row + 1, b * width_out : (b + 1) * width_out] = seen[b]
-    for c in range(3):
-        block = jnp.concatenate([weight_ref[26 - 3 * ab - c] for ab in range(9)], axis=0)
-        taps_ref[c * width_in : (c + 1) * width_in] = block.T
-    taps = taps_ref[...]
-    for out_ref, owner in ((other_ref, 1 - core), (mine_ref, core)):
-        for slot in range(slots):
-            parts = correlate_rows(taps, spread_ref, 2 * rows * slot + rows * owner, width_in)
+        while 4 * done + 4 < 2 * slot + 2 or (slot == 2 * slots - 1 and done < slots):
+            pairs = [correlate_rows(taps, spread_ref, 4 * done + 2 * k, width_in) for k in range(2)]
             for k in range(rows):
-                out_ref[slot, k] = parts[k]
+                owner = OVER_CO.index(done)
+                mine_ref[owner, k] = jnp.where(core == 0, pairs[0][k], pairs[1][k])
+                other_ref[owner, k] = jnp.where(core == 0, pairs[1][k], pairs[0][k])
+            done += 1
 
 
 def add_pair(mine_ref, other_ref, out_ref):
@@ -371,7 +380,7 @@
     )(side, *(stay(x, pltpu.HBM) for x in (features, taps, bias_vector.reshape(1, width_out))))
     both = ("ci", "sp")
     partial, cotangent_other = lax.optimization_barrier((partial, cotangent_other))
-    shares = lax.all_to_all(partial, both, 0, 0, tiled=True)
+    shares = lax.all_to_all(partial, both, 0, 0, tiled=True, axis_index_groups=[OVER_CI_SP])
     acted, copies = call(
         pointwise,
         (pltpu.VMEM((2, 2, width_out, LANES), BF16), pltpu.VMEM(block, BF16)),
@@ -379,7 +388,7 @@
         0,
         2 * size * width_out,
     )(side, shares, bias_columns, cotangent, cotangent_other)
-    gathered = lax.all_to_all(copies, both, 0, 0, tiled=True)
+    gathered = lax.all_to_all(copies, both, 0, 0, tiled=True, axis_index_groups=[OVER_CI_SP])
     quarter = (n_co // 2, rows_y // n_co, width_in, LANES)
     mine, other_half, spread = call(
         backward,
@@ -409,7 +418,7 @@
     summed = call(
         add_pair, pltpu.VMEM(quarter, BF16), [VMEM, VMEM], 0, size * width_in
     )(mine, received)
-    same_core = [list(range(k, n_co, 2)) for k in range(2)]
+    same_core = [[2 * k + core_at for k in OVER_CO] for core_at in range(2)]
     shares = lax.all_to_all(summed, "co", 0, 0, tiled=True, axis_index_groups=same_core)
     other = lax.ppermute(packed, "sp", swap)
     input_grad, weight_grad, bias_grad, activated = call(

time: 60.7 us -> 60.2 us (level); the launches traced: 60.4 us -> 59.2 us
  blocking collectives: 47 us -> 45.2 us
  starting transfers between devices: 6.47 us -> 7.22 us
    all_to_all x2, blocking collectives: 33.1 us -> 30.8 us  [the longest x1 16.3 us: local(): lax.all_to_all(partial, both, 0, 0, tiled=True, axis_index_groups=[OVER_C...]
where the time goes in v5:
time: 60.2 us; the launch traced here: 59.2 us
  blocking collectives  45.2 us (75%)
  starting transfers between devices  7.22 us (12%)
  Pallas kernels  5.98 us (10%)
  between operations  0.68 us (1%)
    all_to_all x1, blocking collectives, local(): lax.all_to_all(partial, both, 0, 0, tiled=True, axis_index_groups=[OVER_C...  16.3 us
    all_to_all x1, blocking collectives, local(): lax.all_to_all(copies, both, 0, 0, tiled=True, axis_index_groups=[OVER_CI...  14.5 us
    all_to_all x1, blocking collectives, local(): lax.all_to_all(summed, 'co', 0, 0, tiled=True, axis_index_groups=same_core)  14.4 us
    ppermute x1, starting transfers between devices, local(): received = lax.ppermute(other_half, 'co', [(k, k ^ 1) for k in range(n_co)])  4.33 us
    pallas_call x1, Pallas kernels, local(): call(forward, (pltpu.VMEM(block, BF16), pltpu.VMEM((width_out, LANES), F3...  2.59 us
    ppermute x1, starting transfers between devices, local(): cotangent_other = lax.ppermute(cotangent, 'sp', swap)  2.13 us
    pallas_call x1, Pallas kernels, local(): call(backward, (pltpu.VMEM(quarter, BF16), pltpu.VMEM(quarter, BF16), plt...  1.24 us
  transfers between devices with their start and end apart: 3, of which 1 were waited for; matrix products, arithmetic and copies ran while one was open for 0% of the time, Pallas kernels for 6%

profile of v5, /device:TPU:1, one launch (start us, length us, event | category | flops | bytes accessed | tf_op | source)
XLA Modules:
  0.0 59.2 jit_solution(464448267649705579)
XLA Ops:
  0.6 2.1 %collective-permute-start = (bf16[4,32,128]{2,1,0:T(8,128)(2,1)}, bf16[4,32,128]{2,1,0:T(8,128)(2,1)S(1)}, u32[]{:S(2)}, u32[]{:S(2)}) collective-permute-start(bf16[4,32,128]{2,1,0:T(8,128)(2,1)} %own_ref.1), channel_id=1, source_target_pairs={{0,1},{1,0},{2,3},{3,2},{4,5},{5,4},{6,7},{7,6},{8,9},{9,8},{10,11... | collective-permute-start | bytes 98312 | tf_op jit(solution)/shard_map/ppermute | solution.py:362
  2.8 2.6 %shard_map.75 = (bf16[16,80,128]{2,1,0:T(8,128)(2,1)S(1)}, f32[32,128]{1,0:T(8,128)S(1)}) custom-call(s32[1]{0:T(128)} %bitcast.side_ref, bf16[32,64,128]{2,1,0:T(8,128)(2,1)} %features_ref.1, bf16[27,32,64]{2,1,0:T(8,128)(2,1)} %bitcast.6, f32[1,32]{1,0:T(1,128)} %bitcast.9), custom_call_target="tpu_custom_call" | custom-call | flops 452984832 | bytes 786432 | tf_op jit(solution)/shard_map/pallas_call | solution.py:364
  5.4 0.0 collective-permute-done.other_ref
  5.4 0.0 copy-start
  5.4 16.3 %all_to_all.15.shares_ref = bf16[16,80,128]{2,1,0:T(8,128)(2,1)S(1)} all-to-all(bf16[16,80,128]{2,1,0:T(8,128)(2,1)S(1)} %get-tuple-element.24), channel_id=1, replica_groups={{0,224,192,160,128,96,64,32,1,225,193,161,129,97,65,33},{2,226,194,162,..., dimensions={0} | all-to-all | bytes 655360 | tf_op jit(solution)/shard_map/all_to_all | solution.py:383
  21.7 0.0 copy-done
  21.7 0.2 shard_map.76
  21.9 0.0 copy-start.2
  21.9 14.5 %all_to_all.16.gathered_ref = bf16[16,80,128]{2,1,0:T(8,128)(2,1)S(1)} all-to-all(bf16[16,80,128]{2,1,0:T(8,128)(2,1)S(1)} %get-tuple-element.27), channel_id=1, replica_groups={{0,224,192,160,128,96,64,32,1,225,193,161,129,97,65,33},{2,226,194,162,..., dimensions={0} | all-to-all | bytes 655360 | tf_op jit(solution)/shard_map/all_to_all | solution.py:391
  36.4 0.0 copy-done.2
  36.4 0.0 copy-start.1
  36.4 1.2 %shard_map.77 = (bf16[8,2,64,128]{3,2,1,0:T(8,128)(2,1)S(1)}, bf16[8,2,64,128]{3,2,1,0:T(8,128)(2,1)S(1)}, bf16[34,96,128]{2,1,0:T(8,128)(2,1)S(1)}) custom-call(s32[1]{0:T(128)} %bitcast.side_ref, s32[1]{0:T(128)} %bitcast.1.core_ref, bf16[16,80,128]{2,1,0:T(8,128)(2,1)S(1)} %all_to_all.16.gathered_ref, bf16[27,32,64]{2,1,0:T(8,128)(2,1)S(1)} %bitcast.7), custom_call_target="tpu_custom_call" | custom-call | flops 452984832 | bytes 786432 | tf_op jit(solution)/shard_map/pallas_call | solution.py:393
  37.6 4.3 %collective-permute-start.1 = (bf16[8,2,64,128]{3,2,1,0:T(8,128)(2,1)S(1)}, bf16[8,2,64,128]{3,2,1,0:T(8,128)(2,1)S(1)}, u32[]{:S(2)}, u32[]{:S(2)}) collective-permute-start(bf16[8,2,64,128]{3,2,1,0:T(8,128)(2,1)S(1)} %get-tuple-element.29), channel_id=1, source_target_pairs={{0,2},{2,0},{4,6},{6,4},{8,10},{10,8},{12,14},{14,12},{16,18},{18,... | collective-permute-start | bytes 786440 | tf_op jit(solution)/shard_map/ppermute | solution.py:416
  42.0 0.0 copy-done.1
  42.0 1.0 %shard_map.78.own_ref = f32[528,128]{1,0:T(8,128)S(1)} custom-call(bf16[32,64,128]{2,1,0:T(8,128)(2,1)S(1)} %copy-done.1, bf16[34,96,128]{2,1,0:T(8,128)(2,1)S(1)} %get-tuple-element.30.spread_ref, bf16[2,2,32,128]{3,2,1,0:T(8,128)(2,1)S(1)} %get-tuple-element.31.act_ref.acted_ref), custom_call_target="tpu_custom_call" | custom-call | flops 452984832 | bytes 786432 | tf_op jit(solution)/shard_map/pallas_call | solution.py:405
  43.0 0.2 collective-permute-done.1.other_ref
  43.1 0.8 %collective-permute-start.2 = (f32[528,128]{1,0:T(8,128)S(1)}, f32[528,128]{1,0:T(8,128)S(1)}, u32[]{:S(2)}, u32[]{:S(2)}) collective-permute-start(f32[528,128]{1,0:T(8,128)S(1)} %shard_map.78.own_ref), channel_id=1, source_target_pairs={{0,1},{1,0},{2,3},{3,2},{4,5},{5,4},{6,7},{7,6},{8,9},{9,8},{10,11... | collective-permute-start | bytes 811016 | tf_op jit(solution)/shard_map/ppermute | solution.py:423
  43.9 0.1 shard_map.79
  44.0 14.4 %all_to_all.17.shares_ref = bf16[8,2,64,128]{3,2,1,0:T(8,128)(2,1)S(1)} all-to-all(bf16[8,2,64,128]{3,2,1,0:T(8,128)(2,1)S(1)} %shard_map.79), channel_id=1, replica_groups={{0,16,4,20,8,24,12,28},{2,18,6,22,10,26,14,30},{1,17,5,21,9,25,13,29},{..., dimensions={0} | all-to-all | bytes 524288 | tf_op jit(solution)/shard_map/all_to_all | solution.py:422
  58.3 0.0 collective-permute-done.2.other_ref
  58.3 0.9 %shard_map.80 = (f32[2,64,128]{2,1,0:T(8,128)}, f32[27,32,64]{2,1,0:T(8,128)}, f32[1,32]{1,0:T(1,128)}, bf16[4,32,128]{2,1,0:T(8,128)(2,1)}) custom-call(s32[1]{0:T(128)} %bitcast.side_ref, bf16[8,2,64,128]{3,2,1,0:T(8,128)(2,1)S(1)} %all_to_all.17.shares_ref, f32[528,128]{1,0:T(8,128)S(1)} %shard_map.78.own_ref, ...), custom_call_target="tpu_custom_call" | custom-call | bytes 221184 | tf_op jit(solution)/shard_map/pallas_call | solution.py:424
Async XLA Ops:
  0.6 4.7 %collective-permute-start = (bf16[4,32,128]{2,1,0:T(8,128)(2,1)}, bf16[4,32,128]{2,1,0:T(8,128)(2,1)S(1)}, u32[]{:S(2)}, u32[]{:S(2)}) collective-permute-start(bf16[4,32,128]{2,1,0:T(8,128)(2,1)} %own_ref.1), channel_id=1, source_target_pairs={{0,1},{1,0},{2,3},{3,2},{4,5},{5,4},{6,7},{7,6},{8,9},{9,8},{10,11... | collective-permute-start | bytes 98312 | tf_op jit(solution)/shard_map/ppermute | solution.py:362
  5.4 16.4 %copy-start = (bf16[4,32,128]{2,1,0:T(8,128)(2,1)S(1)}, bf16[4,32,128]{2,1,0:T(8,128)(2,1)}, u32[]{:S(2)}) copy-start(bf16[4,32,128]{2,1,0:T(8,128)(2,1)} %own_ref.1) | copy-start | bytes 98308
  21.9 14.5 %copy-start.2 = (bf16[27,64,32]{1,2,0:T(8,128)(2,1)S(1)}, bf16[27,64,32]{1,2,0:T(8,128)(2,1)}, u32[]{:S(2)}) copy-start(bf16[27,64,32]{1,2,0:T(8,128)(2,1)} %param.5) | copy-start | bytes 331780
  36.4 5.6 %copy-start.1 = (bf16[32,64,128]{2,1,0:T(8,128)(2,1)S(1)}, bf16[32,64,128]{2,1,0:T(8,128)(2,1)}, u32[]{:S(2)}) copy-start(bf16[32,64,128]{2,1,0:T(8,128)(2,1)} %features_ref.1) | copy-start | bytes 1572868
  37.6 5.5 %collective-permute-start.1 = (bf16[8,2,64,128]{3,2,1,0:T(8,128)(2,1)S(1)}, bf16[8,2,64,128]{3,2,1,0:T(8,128)(2,1)S(1)}, u32[]{:S(2)}, u32[]{:S(2)}) collective-permute-start(bf16[8,2,64,128]{3,2,1,0:T(8,128)(2,1)S(1)} %get-tuple-element.29), channel_id=1, source_target_pairs={{0,2},{2,0},{4,6},{6,4},{8,10},{10,8},{12,14},{14,12},{16,18},{18,... | collective-permute-start | bytes 786440 | tf_op jit(solution)/shard_map/ppermute | solution.py:416
  43.1 15.2 %collective-permute-start.2 = (f32[528,128]{1,0:T(8,128)S(1)}, f32[528,128]{1,0:T(8,128)S(1)}, u32[]{:S(2)}, u32[]{:S(2)}) collective-permute-start(f32[528,128]{1,0:T(8,128)S(1)} %shard_map.78.own_ref), channel_id=1, source_target_pairs={{0,1},{1,0},{2,3},{3,2},{4,5},{5,4},{6,7},{7,6},{8,9},{9,8},{10,11... | collective-permute-start | bytes 811016 | tf_op jit(solution)/shard_map/ppermute | solution.py:423

commit v6 on v5

--- a/solution.py
+++ b/solution.py
@@ -84,10 +84,18 @@
     return parts
 
 
-def correlate_rows(taps, spread_ref, y, width):
-    depth = 3 * spread_ref.shape[1]
+def correlate_rows(taps, spread_ref, y, width, own_ref=None):
+    def row(at):
+        rows = spread_ref[at]
+        if own_ref is None:
+            return [rows]
+        inside = 1 <= at <= own_ref.shape[0]
+        own = own_ref[at - 1] if inside else jnp.zeros(own_ref.shape[1:], BF16)
+        return [rows[: own.shape[0]], own, rows[own.shape[0] :]]
+
     columns = jnp.concatenate(
-        [spread_ref[y + k : y + k + 3].reshape(depth, LANES) for k in range(2)], axis=1
+        [jnp.concatenate(sum((row(y + k + a) for a in range(3)), []), axis=0) for k in range(2)],
+        axis=1,
     )
     product = jnp.dot(taps, columns, preferred_element_type=F32)
     parts = along_z([product[c * width : (c + 1) * width] for c in range(3)])
@@ -102,10 +110,19 @@
     width_out = weight_ref.shape[1]
     groups = rows_y // 4
     fetch_weight = pltpu.make_async_copy(weight_hbm, weight_ref, sems.at[0])
-    fetch = pltpu.make_async_copy(features_hbm, features_ref, sems.at[1])
-    fetch_bias = pltpu.make_async_copy(bias_hbm, bias_ref, sems.at[2])
+    step = rows_y // 2
+    fetch = [
+        pltpu.make_async_copy(
+            features_hbm.at[pl.ds(k * step, step)],
+            features_ref.at[pl.ds(k * step, step)],
+            sems.at[2 + k],
+        )
+        for k in range(2)
+    ]
+    fetch_bias = pltpu.make_async_copy(bias_hbm, bias_ref, sems.at[1])
     fetch_weight.start()
-    fetch.start()
+    for copy in fetch:
+        copy.start()
     fetch_bias.start()
     side = side_ref[0]
     blank = jnp.zeros(spread_ref.shape[1:], BF16)
@@ -124,17 +141,18 @@
     diagonal = lax.broadcasted_iota(jnp.int32, shape, 0) == lane(shape)
     column = jnp.sum(jnp.where(diagonal, bias_ref[...], 0.0), axis=1, keepdims=True)
     column_ref[...] = jnp.broadcast_to(column, column_ref.shape)
-    fetch.wait()
+    for copy in fetch:
+        copy.wait()
     done = 0
     for group in range(groups):
         planes = [features_ref[4 * group + k] for k in range(4)]
         for k in range(4):
             seen = neighbours(planes[k])
-            for b in range(3):
-                spread_ref[4 * group + k + 1, b * width_in : (b + 1) * width_in] = seen[b]
+            for b in (0, 2):
+                spread_ref[4 * group + k + 1, b // 2 * width_in : (b // 2 + 1) * width_in] = seen[b]
         edge_ref[group + 1] = pack_plane(side, planes)
         while done + 2 < 4 * group or (group == groups - 1 and done < rows_y):
-            parts = correlate_rows(taps, spread_ref, done, width_out)
+            parts = correlate_rows(taps, spread_ref, done, width_out, features_ref)
             for k in range(2):
                 place = OVER_CI_SP.index(done // 2)
                 out_ref[place, k * width_out : (k + 1) * width_out] = parts[k]
@@ -371,11 +389,11 @@
             pltpu.VMEM(features.shape, BF16),
             pltpu.VMEM(taps.shape, BF16),
             pltpu.VMEM((1, width_out), F32),
-            pltpu.VMEM((rows_y + 2, 3 * width_in, LANES), BF16),
+            pltpu.VMEM((rows_y + 2, 2 * width_in, LANES), BF16),
             pltpu.VMEM((3 * width_out, 9 * width_in), BF16),
             pltpu.VMEM((3 * width_out, 3 * width_in), BF16),
             pltpu.VMEM((rows_y // 4 + 2, width_in, LANES), BF16),
-            pltpu.SemaphoreType.DMA((3,)),
+            pltpu.SemaphoreType.DMA((4,)),
         ],
     )(side, *(stay(x, pltpu.HBM) for x in (features, taps, bias_vector.reshape(1, width_out))))
     both = ("ci", "sp")

time: 60.2 us -> 60.2 us (level)
  no operation moved by 1% of the time
where the time goes in v6:
time: 60.2 us; the launch traced here: 59.1 us
  blocking collectives  45.1 us (75%)
  starting transfers between devices  7.22 us (12%)
  Pallas kernels  5.93 us (10%)
  between operations  0.68 us (1%)
    all_to_all x1, blocking collectives, local(): lax.all_to_all(partial, both, 0, 0, tiled=True, axis_index_groups=[OVER_C...  16.4 us
    all_to_all x1, blocking collectives, local(): lax.all_to_all(copies, both, 0, 0, tiled=True, axis_index_groups=[OVER_CI...  14.5 us
    all_to_all x1, blocking collectives, local(): lax.all_to_all(summed, 'co', 0, 0, tiled=True, axis_index_groups=same_core)  14.2 us
    ppermute x1, starting transfers between devices, local(): received = lax.ppermute(other_half, 'co', [(k, k ^ 1) for k in range(n_co)])  4.33 us
    pallas_call x1, Pallas kernels, local(): call(forward, (pltpu.VMEM(block, BF16), pltpu.VMEM((width_out, LANES), F3...  2.54 us
    ppermute x1, starting transfers between devices, local(): cotangent_other = lax.ppermute(cotangent, 'sp', swap)  2.13 us
    pallas_call x1, Pallas kernels, local(): call(backward, (pltpu.VMEM(quarter, BF16), pltpu.VMEM(quarter, BF16), plt...  1.24 us
  transfers between devices with their start and end apart: 3, of which 1 were waited for; matrix products, arithmetic and copies ran while one was open for 0% of the time, Pallas kernels for 6%

profile of v6, /device:TPU:1, one launch (start us, length us, event | category | flops | bytes accessed | tf_op | source)
XLA Modules:
  0.0 59.1 jit_solution(15954202685193620982)
XLA Ops:
  0.6 2.1 %collective-permute-start = (bf16[4,32,128]{2,1,0:T(8,128)(2,1)}, bf16[4,32,128]{2,1,0:T(8,128)(2,1)S(1)}, u32[]{:S(2)}, u32[]{:S(2)}) collective-permute-start(bf16[4,32,128]{2,1,0:T(8,128)(2,1)} %own_ref.1), channel_id=1, source_target_pairs={{0,1},{1,0},{2,3},{3,2},{4,5},{5,4},{6,7},{7,6},{8,9},{9,8},{10,11... | collective-permute-start | bytes 98312 | tf_op jit(solution)/shard_map/ppermute | solution.py:380
  2.8 2.5 %shard_map.75 = (bf16[16,80,128]{2,1,0:T(8,128)(2,1)S(1)}, f32[32,128]{1,0:T(8,128)S(1)}) custom-call(s32[1]{0:T(128)} %bitcast.side_ref, bf16[32,64,128]{2,1,0:T(8,128)(2,1)} %features_ref.1, bf16[27,32,64]{2,1,0:T(8,128)(2,1)} %bitcast.6, f32[1,32]{1,0:T(1,128)} %bitcast.9), custom_call_target="tpu_custom_call" | custom-call | flops 452984832 | bytes 786432 | tf_op jit(solution)/shard_map/pallas_call | solution.py:382
  5.3 0.0 collective-permute-done.other_ref
  5.3 0.0 copy-start
  5.3 16.4 %all_to_all.15.shares_ref = bf16[16,80,128]{2,1,0:T(8,128)(2,1)S(1)} all-to-all(bf16[16,80,128]{2,1,0:T(8,128)(2,1)S(1)} %get-tuple-element.24), channel_id=1, replica_groups={{0,224,192,160,128,96,64,32,1,225,193,161,129,97,65,33},{2,226,194,162,..., dimensions={0} | all-to-all | bytes 655360 | tf_op jit(solution)/shard_map/all_to_all | solution.py:401
  21.7 0.0 copy-done
  21.7 0.2 shard_map.76
  21.9 0.0 copy-start.2
  21.9 14.5 %all_to_all.16.gathered_ref = bf16[16,80,128]{2,1,0:T(8,128)(2,1)S(1)} all-to-all(bf16[16,80,128]{2,1,0:T(8,128)(2,1)S(1)} %get-tuple-element.27), channel_id=1, replica_groups={{0,224,192,160,128,96,64,32,1,225,193,161,129,97,65,33},{2,226,194,162,..., dimensions={0} | all-to-all | bytes 655360 | tf_op jit(solution)/shard_map/all_to_all | solution.py:409
  36.4 0.0 copy-done.2
  36.4 0.0 copy-start.1
  36.4 1.2 %shard_map.77 = (bf16[8,2,64,128]{3,2,1,0:T(8,128)(2,1)S(1)}, bf16[8,2,64,128]{3,2,1,0:T(8,128)(2,1)S(1)}, bf16[34,96,128]{2,1,0:T(8,128)(2,1)S(1)}) custom-call(s32[1]{0:T(128)} %bitcast.side_ref, s32[1]{0:T(128)} %bitcast.1.core_ref, bf16[16,80,128]{2,1,0:T(8,128)(2,1)S(1)} %all_to_all.16.gathered_ref, bf16[27,32,64]{2,1,0:T(8,128)(2,1)S(1)} %bitcast.7), custom_call_target="tpu_custom_call" | custom-call | flops 452984832 | bytes 786432 | tf_op jit(solution)/shard_map/pallas_call | solution.py:411
  37.6 4.3 %collective-permute-start.1 = (bf16[8,2,64,128]{3,2,1,0:T(8,128)(2,1)S(1)}, bf16[8,2,64,128]{3,2,1,0:T(8,128)(2,1)S(1)}, u32[]{:S(2)}, u32[]{:S(2)}) collective-permute-start(bf16[8,2,64,128]{3,2,1,0:T(8,128)(2,1)S(1)} %get-tuple-element.29), channel_id=1, source_target_pairs={{0,2},{2,0},{4,6},{6,4},{8,10},{10,8},{12,14},{14,12},{16,18},{18,... | collective-permute-start | bytes 786440 | tf_op jit(solution)/shard_map/ppermute | solution.py:434
  42.0 0.0 copy-done.1
  42.0 1.0 %shard_map.78.own_ref = f32[528,128]{1,0:T(8,128)S(1)} custom-call(bf16[32,64,128]{2,1,0:T(8,128)(2,1)S(1)} %copy-done.1, bf16[34,96,128]{2,1,0:T(8,128)(2,1)S(1)} %get-tuple-element.30.spread_ref, bf16[2,2,32,128]{3,2,1,0:T(8,128)(2,1)S(1)} %get-tuple-element.31.act_ref.acted_ref), custom_call_target="tpu_custom_call" | custom-call | flops 452984832 | bytes 786432 | tf_op jit(solution)/shard_map/pallas_call | solution.py:423
  43.0 0.2 collective-permute-done.1.other_ref
  43.1 0.8 %collective-permute-start.2 = (f32[528,128]{1,0:T(8,128)S(1)}, f32[528,128]{1,0:T(8,128)S(1)}, u32[]{:S(2)}, u32[]{:S(2)}) collective-permute-start(f32[528,128]{1,0:T(8,128)S(1)} %shard_map.78.own_ref), channel_id=1, source_target_pairs={{0,1},{1,0},{2,3},{3,2},{4,5},{5,4},{6,7},{7,6},{8,9},{9,8},{10,11... | collective-permute-start | bytes 811016 | tf_op jit(solution)/shard_map/ppermute | solution.py:441
  43.9 0.1 shard_map.79
  44.0 14.2 %all_to_all.17.shares_ref = bf16[8,2,64,128]{3,2,1,0:T(8,128)(2,1)S(1)} all-to-all(bf16[8,2,64,128]{3,2,1,0:T(8,128)(2,1)S(1)} %shard_map.79), channel_id=1, replica_groups={{0,16,4,20,8,24,12,28},{2,18,6,22,10,26,14,30},{1,17,5,21,9,25,13,29},{..., dimensions={0} | all-to-all | bytes 524288 | tf_op jit(solution)/shard_map/all_to_all | solution.py:440
  58.2 0.0 collective-permute-done.2.other_ref
  58.2 0.9 %shard_map.80 = (f32[2,64,128]{2,1,0:T(8,128)}, f32[27,32,64]{2,1,0:T(8,128)}, f32[1,32]{1,0:T(1,128)}, bf16[4,32,128]{2,1,0:T(8,128)(2,1)}) custom-call(s32[1]{0:T(128)} %bitcast.side_ref, bf16[8,2,64,128]{3,2,1,0:T(8,128)(2,1)S(1)} %all_to_all.17.shares_ref, f32[528,128]{1,0:T(8,128)S(1)} %shard_map.78.own_ref, ...), custom_call_target="tpu_custom_call" | custom-call | bytes 221184 | tf_op jit(solution)/shard_map/pallas_call | solution.py:442
Async XLA Ops:
  0.6 4.7 %collective-permute-start = (bf16[4,32,128]{2,1,0:T(8,128)(2,1)}, bf16[4,32,128]{2,1,0:T(8,128)(2,1)S(1)}, u32[]{:S(2)}, u32[]{:S(2)}) collective-permute-start(bf16[4,32,128]{2,1,0:T(8,128)(2,1)} %own_ref.1), channel_id=1, source_target_pairs={{0,1},{1,0},{2,3},{3,2},{4,5},{5,4},{6,7},{7,6},{8,9},{9,8},{10,11... | collective-permute-start | bytes 98312 | tf_op jit(solution)/shard_map/ppermute | solution.py:380
  5.3 16.4 %copy-start = (bf16[4,32,128]{2,1,0:T(8,128)(2,1)S(1)}, bf16[4,32,128]{2,1,0:T(8,128)(2,1)}, u32[]{:S(2)}) copy-start(bf16[4,32,128]{2,1,0:T(8,128)(2,1)} %own_ref.1) | copy-start | bytes 98308
  21.9 14.5 %copy-start.2 = (bf16[27,64,32]{1,2,0:T(8,128)(2,1)S(1)}, bf16[27,64,32]{1,2,0:T(8,128)(2,1)}, u32[]{:S(2)}) copy-start(bf16[27,64,32]{1,2,0:T(8,128)(2,1)} %param.5) | copy-start | bytes 331780
  36.4 5.6 %copy-start.1 = (bf16[32,64,128]{2,1,0:T(8,128)(2,1)S(1)}, bf16[32,64,128]{2,1,0:T(8,128)(2,1)}, u32[]{:S(2)}) copy-start(bf16[32,64,128]{2,1,0:T(8,128)(2,1)} %features_ref.1) | copy-start | bytes 1572868
  37.6 5.5 %collective-permute-start.1 = (bf16[8,2,64,128]{3,2,1,0:T(8,128)(2,1)S(1)}, bf16[8,2,64,128]{3,2,1,0:T(8,128)(2,1)S(1)}, u32[]{:S(2)}, u32[]{:S(2)}) collective-permute-start(bf16[8,2,64,128]{3,2,1,0:T(8,128)(2,1)S(1)} %get-tuple-element.29), channel_id=1, source_target_pairs={{0,2},{2,0},{4,6},{6,4},{8,10},{10,8},{12,14},{14,12},{16,18},{18,... | collective-permute-start | bytes 786440 | tf_op jit(solution)/shard_map/ppermute | solution.py:434
  43.1 15.0 %collective-permute-start.2 = (f32[528,128]{1,0:T(8,128)S(1)}, f32[528,128]{1,0:T(8,128)S(1)}, u32[]{:S(2)}, u32[]{:S(2)}) collective-permute-start(f32[528,128]{1,0:T(8,128)S(1)} %shard_map.78.own_ref), channel_id=1, source_target_pairs={{0,1},{1,0},{2,3},{3,2},{4,5},{5,4},{6,7},{7,6},{8,9},{9,8},{10,11... | collective-permute-start | bytes 811016 | tf_op jit(solution)/shard_map/ppermute | solution.py:441

commit v7 on v6

--- a/solution.py
+++ b/solution.py
@@ -103,7 +103,7 @@
 
 
 def forward(
-    side_ref, features_hbm, weight_hbm, bias_hbm, out_ref, column_ref,
+    side_ref, core_ref, features_hbm, weight_hbm, bias_hbm, out_ref, column_ref, flipped_ref,
     features_ref, weight_ref, bias_ref, spread_ref, taps_ref, edge_taps_ref, edge_ref, sems,
 ):
     rows_y, width_in, _ = features_ref.shape
@@ -135,6 +135,10 @@
         edge_taps_ref[rows] = jnp.concatenate(
             [weight_ref[9 * a + c + 6 * side] for a in range(3)], axis=1
         )
+    @pl.when(core_ref[0] == 0)
+    def _():
+        flip_taps(weight_ref, flipped_ref)
+
     taps = taps_ref[...]
     fetch_bias.wait()
     shape = (width_out, width_out)
@@ -235,8 +239,16 @@
         out_ref[k] = blocks[OVER_CI_SP[k] % 2]
 
 
+def flip_taps(weight_ref, taps_ref):
+    width_in = weight_ref.shape[2]
+    for c in range(3):
+        block = jnp.concatenate([weight_ref[26 - 3 * ab - c] for ab in range(9)], axis=0)
+        taps_ref[c * width_in : (c + 1) * width_in] = block.T
+
+
 def backward(
-    side_ref, core_ref, gathered_ref, weight_ref, mine_ref, other_ref, spread_ref, taps_ref,
+    side_ref, core_ref, gathered_ref, weight_ref, flipped_ref,
+    mine_ref, other_ref, spread_ref, taps_ref,
 ):
     slots, rows, width_in, _ = mine_ref.shape
     rows_y = 2 * slots * rows
@@ -246,9 +258,15 @@
     spread_ref[0] = blank
     spread_ref[rows_y + 1] = blank
 
-    for c in range(3):
-        block = jnp.concatenate([weight_ref[26 - 3 * ab - c] for ab in range(9)], axis=0)
-        taps_ref[c * width_in : (c + 1) * width_in] = block.T
+
+    @pl.when(core == 0)
+    def _():
+        taps_ref[...] = flipped_ref[...]
+
+    @pl.when(core == 1)
+    def _():
+        flip_taps(weight_ref, taps_ref)
+
     taps = taps_ref[...]
     side = side_ref[0]
     half, at = width_out // 2, lane((width_out, LANES))
@@ -379,10 +397,14 @@
 
     cotangent_other = lax.ppermute(cotangent, "sp", swap)
     block = (2 * n_ci, 2 * width_out + width_out // 2, LANES)
-    partial, bias_columns = call(
+    partial, bias_columns, flipped = call(
         forward,
-        (pltpu.VMEM(block, BF16), pltpu.VMEM((width_out, LANES), F32)),
-        [SMEM, HBM, HBM, HBM],
+        (
+            pltpu.VMEM(block, BF16),
+            pltpu.VMEM((width_out, LANES), F32),
+            pltpu.VMEM((3 * width_in, 9 * width_out), BF16),
+        ),
+        [SMEM, SMEM, HBM, HBM, HBM],
         work,
         size * (width_in + width_out),
         [
@@ -395,7 +417,7 @@
             pltpu.VMEM((rows_y // 4 + 2, width_in, LANES), BF16),
             pltpu.SemaphoreType.DMA((4,)),
         ],
-    )(side, *(stay(x, pltpu.HBM) for x in (features, taps, bias_vector.reshape(1, width_out))))
+    )(side, core, *(stay(x, pltpu.HBM) for x in (features, taps, bias_vector.reshape(1, width_out))))
     both = ("ci", "sp")
     partial, cotangent_other = lax.optimization_barrier((partial, cotangent_other))
     shares = lax.all_to_all(partial, both, 0, 0, tiled=True, axis_index_groups=[OVER_CI_SP])
@@ -415,11 +437,11 @@
             pltpu.VMEM(quarter, BF16),
             pltpu.VMEM((rows_y + 2, 3 * width_out, LANES), BF16),
         ),
-        [SMEM, SMEM, VMEM, VMEM],
+        [SMEM, SMEM, VMEM, VMEM, VMEM],
         work,
         size * (width_in + width_out),
         [pltpu.VMEM((3 * width_in, 9 * width_out), BF16)],
-    )(side, core, gathered, taps)
+    )(side, core, gathered, taps, flipped)
     packed = call(
         filter_gradient,
         shape((9 * width_out + 9 * width_out // 2 + 3 * width_out, LANES), F32),

time: 60.2 us -> 60.1 us (level)
  no operation moved by 1% of the time
where the time goes in v7:
time: 60.1 us; the launch traced here: 59 us
  blocking collectives  45.1 us (75%)
  starting transfers between devices  7.11 us (12%)
  Pallas kernels  6 us (10%)
  between operations  0.68 us (1%)
    all_to_all x1, blocking collectives, local(): lax.all_to_all(partial, both, 0, 0, tiled=True, axis_index_groups=[OVER_C...  16.4 us
    all_to_all x1, blocking collectives, local(): lax.all_to_all(copies, both, 0, 0, tiled=True, axis_index_groups=[OVER_CI...  14.5 us
    all_to_all x1, blocking collectives, local(): lax.all_to_all(summed, 'co', 0, 0, tiled=True, axis_index_groups=same_core)  14.2 us
    ppermute x1, starting transfers between devices, local(): received = lax.ppermute(other_half, 'co', [(k, k ^ 1) for k in range(n_co)])  4.22 us
    pallas_call x1, Pallas kernels, local(): call(forward, (pltpu.VMEM(block, BF16), pltpu.VMEM((width_out, LANES), F3...  2.54 us
    ppermute x1, starting transfers between devices, local(): cotangent_other = lax.ppermute(cotangent, 'sp', swap)  2.13 us
    pallas_call x1, Pallas kernels, local(): call(backward, (pltpu.VMEM(quarter, BF16), pltpu.VMEM(quarter, BF16), plt...  1.3 us
  transfers between devices with their start and end apart: 3, of which 1 were waited for; matrix products, arithmetic and copies ran while one was open for 0% of the time, Pallas kernels for 6%

profile of v7, /device:TPU:1, one launch (start us, length us, event | category | flops | bytes accessed | tf_op | source)
XLA Modules:
  0.0 59.0 jit_solution(11619129063567682150)
XLA Ops:
  0.6 2.1 %collective-permute-start = (bf16[4,32,128]{2,1,0:T(8,128)(2,1)}, bf16[4,32,128]{2,1,0:T(8,128)(2,1)S(1)}, u32[]{:S(2)}, u32[]{:S(2)}) collective-permute-start(bf16[4,32,128]{2,1,0:T(8,128)(2,1)} %own_ref.1), channel_id=1, source_target_pairs={{0,1},{1,0},{2,3},{3,2},{4,5},{5,4},{6,7},{7,6},{8,9},{9,8},{10,11... | collective-permute-start | bytes 98312 | tf_op jit(solution)/shard_map/ppermute | solution.py:398
  2.8 2.5 %shard_map.75 = (bf16[16,80,128]{2,1,0:T(8,128)(2,1)S(1)}, f32[32,128]{1,0:T(8,128)S(1)}, bf16[192,288]{1,0:T(8,128)(2,1)S(1)}) custom-call(s32[1]{0:T(128)} %bitcast.side_ref, s32[1]{0:T(128)} %bitcast.1.core_ref, bf16[32,64,128]{2,1,0:T(8,128)(2,1)} %features_ref.1, bf16[27,32,64]{2,1,0:T(8,128)(2,1)} %bitcast.6, f32[1,32]{1,0:T(1,128)} %bitcast.9), custom_call_target="tpu_custom_call" | custom-call | flops 452984832 | bytes 786432 | tf_op jit(solution)/shard_map/pallas_call | solution.py:400
  5.3 0.0 collective-permute-done.other_ref
  5.3 0.0 copy-start
  5.3 16.4 %all_to_all.15.shares_ref = bf16[16,80,128]{2,1,0:T(8,128)(2,1)S(1)} all-to-all(bf16[16,80,128]{2,1,0:T(8,128)(2,1)S(1)} %get-tuple-element.25), channel_id=1, replica_groups={{0,224,192,160,128,96,64,32,1,225,193,161,129,97,65,33},{2,226,194,162,..., dimensions={0} | all-to-all | bytes 655360 | tf_op jit(solution)/shard_map/all_to_all | solution.py:423
  21.7 0.0 copy-done
  21.7 0.2 shard_map.76
  21.9 0.0 copy-start.2
  21.9 14.5 %all_to_all.16.gathered_ref = bf16[16,80,128]{2,1,0:T(8,128)(2,1)S(1)} all-to-all(bf16[16,80,128]{2,1,0:T(8,128)(2,1)S(1)} %get-tuple-element.28), channel_id=1, replica_groups={{0,224,192,160,128,96,64,32,1,225,193,161,129,97,65,33},{2,226,194,162,..., dimensions={0} | all-to-all | bytes 655360 | tf_op jit(solution)/shard_map/all_to_all | solution.py:431
  36.4 0.0 copy-done.2
  36.4 0.0 copy-start.1
  36.4 1.3 %shard_map.77 = (bf16[8,2,64,128]{3,2,1,0:T(8,128)(2,1)S(1)}, bf16[8,2,64,128]{3,2,1,0:T(8,128)(2,1)S(1)}, bf16[34,96,128]{2,1,0:T(8,128)(2,1)S(1)}) custom-call(s32[1]{0:T(128)} %bitcast.side_ref, s32[1]{0:T(128)} %bitcast.1.core_ref, bf16[16,80,128]{2,1,0:T(8,128)(2,1)S(1)} %all_to_all.16.gathered_ref, bf16[27,32,64]{2,1,0:T(8,128)(2,1)S(1)} %bitcast.7, ...), custom_call_target="tpu_custom_call" | custom-call | flops 452984832 | bytes 786432 | tf_op jit(solution)/shard_map/pallas_call | solution.py:433
  37.7 4.2 %collective-permute-start.1 = (bf16[8,2,64,128]{3,2,1,0:T(8,128)(2,1)S(1)}, bf16[8,2,64,128]{3,2,1,0:T(8,128)(2,1)S(1)}, u32[]{:S(2)}, u32[]{:S(2)}) collective-permute-start(bf16[8,2,64,128]{3,2,1,0:T(8,128)(2,1)S(1)} %get-tuple-element.31), channel_id=1, source_target_pairs={{0,2},{2,0},{4,6},{6,4},{8,10},{10,8},{12,14},{14,12},{16,18},{18,... | collective-permute-start | bytes 786440 | tf_op jit(solution)/shard_map/ppermute | solution.py:456
  41.9 0.0 copy-done.1
  41.9 1.0 %shard_map.78.own_ref = f32[528,128]{1,0:T(8,128)S(1)} custom-call(bf16[32,64,128]{2,1,0:T(8,128)(2,1)S(1)} %copy-done.1, bf16[34,96,128]{2,1,0:T(8,128)(2,1)S(1)} %get-tuple-element.32.spread_ref, bf16[2,2,32,128]{3,2,1,0:T(8,128)(2,1)S(1)} %get-tuple-element.33.act_ref.acted_ref), custom_call_target="tpu_custom_call" | custom-call | flops 452984832 | bytes 786432 | tf_op jit(solution)/shard_map/pallas_call | solution.py:445
  42.9 0.2 collective-permute-done.1.other_ref
  43.1 0.8 %collective-permute-start.2 = (f32[528,128]{1,0:T(8,128)S(1)}, f32[528,128]{1,0:T(8,128)S(1)}, u32[]{:S(2)}, u32[]{:S(2)}) collective-permute-start(f32[528,128]{1,0:T(8,128)S(1)} %shard_map.78.own_ref), channel_id=1, source_target_pairs={{0,1},{1,0},{2,3},{3,2},{4,5},{5,4},{6,7},{7,6},{8,9},{9,8},{10,11... | collective-permute-start | bytes 811016 | tf_op jit(solution)/shard_map/ppermute | solution.py:463
  43.9 0.1 shard_map.79
  43.9 14.2 %all_to_all.17.shares_ref = bf16[8,2,64,128]{3,2,1,0:T(8,128)(2,1)S(1)} all-to-all(bf16[8,2,64,128]{3,2,1,0:T(8,128)(2,1)S(1)} %shard_map.79), channel_id=1, replica_groups={{0,16,4,20,8,24,12,28},{2,18,6,22,10,26,14,30},{1,17,5,21,9,25,13,29},{..., dimensions={0} | all-to-all | bytes 524288 | tf_op jit(solution)/shard_map/all_to_all | solution.py:462
  58.1 0.0 collective-permute-done.2.other_ref
  58.1 0.9 %shard_map.80 = (f32[2,64,128]{2,1,0:T(8,128)}, f32[27,32,64]{2,1,0:T(8,128)}, f32[1,32]{1,0:T(1,128)}, bf16[4,32,128]{2,1,0:T(8,128)(2,1)}) custom-call(s32[1]{0:T(128)} %bitcast.side_ref, bf16[8,2,64,128]{3,2,1,0:T(8,128)(2,1)S(1)} %all_to_all.17.shares_ref, f32[528,128]{1,0:T(8,128)S(1)} %shard_map.78.own_ref, ...), custom_call_target="tpu_custom_call" | custom-call | bytes 221184 | tf_op jit(solution)/shard_map/pallas_call | solution.py:464
Async XLA Ops:
  0.6 4.7 %collective-permute-start = (bf16[4,32,128]{2,1,0:T(8,128)(2,1)}, bf16[4,32,128]{2,1,0:T(8,128)(2,1)S(1)}, u32[]{:S(2)}, u32[]{:S(2)}) collective-permute-start(bf16[4,32,128]{2,1,0:T(8,128)(2,1)} %own_ref.1), channel_id=1, source_target_pairs={{0,1},{1,0},{2,3},{3,2},{4,5},{5,4},{6,7},{7,6},{8,9},{9,8},{10,11... | collective-permute-start | bytes 98312 | tf_op jit(solution)/shard_map/ppermute | solution.py:398
  5.3 16.4 %copy-start = (bf16[4,32,128]{2,1,0:T(8,128)(2,1)S(1)}, bf16[4,32,128]{2,1,0:T(8,128)(2,1)}, u32[]{:S(2)}) copy-start(bf16[4,32,128]{2,1,0:T(8,128)(2,1)} %own_ref.1) | copy-start | bytes 98308
  21.9 14.5 %copy-start.2 = (bf16[27,64,32]{1,2,0:T(8,128)(2,1)S(1)}, bf16[27,64,32]{1,2,0:T(8,128)(2,1)}, u32[]{:S(2)}) copy-start(bf16[27,64,32]{1,2,0:T(8,128)(2,1)} %param.5) | copy-start | bytes 331780
  36.4 5.5 %copy-start.1 = (bf16[32,64,128]{2,1,0:T(8,128)(2,1)S(1)}, bf16[32,64,128]{2,1,0:T(8,128)(2,1)}, u32[]{:S(2)}) copy-start(bf16[32,64,128]{2,1,0:T(8,128)(2,1)} %features_ref.1) | copy-start | bytes 1572868
  37.7 5.4 %collective-permute-start.1 = (bf16[8,2,64,128]{3,2,1,0:T(8,128)(2,1)S(1)}, bf16[8,2,64,128]{3,2,1,0:T(8,128)(2,1)S(1)}, u32[]{:S(2)}, u32[]{:S(2)}) collective-permute-start(bf16[8,2,64,128]{3,2,1,0:T(8,128)(2,1)S(1)} %get-tuple-element.31), channel_id=1, source_target_pairs={{0,2},{2,0},{4,6},{6,4},{8,10},{10,8},{12,14},{14,12},{16,18},{18,... | collective-permute-start | bytes 786440 | tf_op jit(solution)/shard_map/ppermute | solution.py:456
  43.1 15.0 %collective-permute-start.2 = (f32[528,128]{1,0:T(8,128)S(1)}, f32[528,128]{1,0:T(8,128)S(1)}, u32[]{:S(2)}, u32[]{:S(2)}) collective-permute-start(f32[528,128]{1,0:T(8,128)S(1)} %shard_map.78.own_ref), channel_id=1, source_target_pairs={{0,1},{1,0},{2,3},{3,2},{4,5},{5,4},{6,7},{7,6},{8,9},{9,8},{10,11... | collective-permute-start | bytes 811016 | tf_op jit(solution)/shard_map/ppermute | solution.py:463
